TPU v7x, 32 devices: a whole 2x2x4 slice. The times are simulated.
32 devices in a mesh: section: 8 (over z, y), dp: 4 (over x, core).
Axes of the slice: x: 2, y: 2, z: 4, core: 2. Of those that a mesh axis runs over, the one named last changes fastest.
Arguments:
- entering: bfloat16 [8, 512, 8192], P('section', 'dp'), may hold values from -6 to 6
- returning: bfloat16 [8, 512, 8192], P('section', 'dp'), may hold values from -6 to 6
- adapter_down: bfloat16 [2, 8, 64, 8192], P(None, 'section'), may hold values from -0.0625 to 0.0625
- adapter_up: bfloat16 [2, 8, 64, 8192], P(None, 'section'), may hold values from -0.75 to 0.75
- stashed: float32 [8, 3, 64, 512], P('section', None, None, 'dp'), may hold values from -6 to 6
- doc_ids: int32 [8, 512], P(None, 'dp'), may hold values from 0 to 7, never falling along the last dimension, each value on 1 to 256 neighbouring positions
- input_factor: float32 [8, 8192, 1024], P('section', 'dp'), may hold values from -3 to 3
- output_factor: float32 [2, 8, 64, 64], P(None, 'section'), may hold values from -3 to 3
Outputs:
- input_factor_new: float32 [8, 8192, 1024], P('section', 'dp')
- output_factor_new: float32 [2, 8, 64, 64], P(None, 'section')
Inputs may be any that keep to these rules, and one draw needn't show every extreme that they name: `doc_ids`: each row packs 8 documents in order: document numbers never fall along a row, every document has 1 to 256 tokens, and some document of every row has exactly 256.
All inputs are finite; a program needn't handle non-finite values.
Results may differ from a plain program's by a relative error of at most 0.0044.
Values may be sent and summed in bfloat16 or wider, within the bound.
A program may use at most 128 MiB of HBM per device.

v0:
```python
import jax
import jax.numpy as jnp
from jax import lax
from jax.sharding import PartitionSpec as P


def from_behind(block, axis, distance):
    devices = range(lax.axis_size(axis))
    route = [((i - distance) % len(devices), i) for i in devices]
    return lax.ppermute(block, axis, route)


def select_span(weights, span_id):
    return lax.dynamic_index_in_dim(weights[:, 0], span_id, 0, keepdims=False)


def shards(
    entering, returning, adapter_down, adapter_up, stashed, doc_ids, input_factor, output_factor
):
    section_index = lax.axis_index("section")
    section_count = lax.axis_size("section")
    replicas = lax.axis_size("dp")
    tok_rows = entering.shape[1]
    model_width = entering.shape[2]
    steps_count = stashed.shape[1]
    block_size = input_factor.shape[2]
    doc_range = jnp.arange(2 * replicas, dtype=jnp.int32)
    onehot = (doc_ids[:, :, None] == doc_range[None, None, :]).astype(jnp.int32)
    local_counts = jnp.sum(onehot, axis=1)
    counts = lax.psum(local_counts, "dp").astype(jnp.float32)
    doc_length = jnp.sum(onehot.astype(jnp.float32) * counts[:, None, :], axis=2)
    weight = jnp.sqrt(tok_rows / doc_length)
    current = entering[0]
    pieces = []
    for step_idx in range(steps_count):
        anchor = (section_index - step_idx) % section_count
        span_id = (anchor < section_count // 2).astype(jnp.int32) + (
            section_index < step_idx
        ).astype(jnp.int32)
        row_scale = jnp.sqrt(lax.dynamic_index_in_dim(weight, anchor, 0, keepdims=False))
        pieces.append((row_scale[:, None] * current.astype(jnp.float32)).astype(jnp.bfloat16))
        if step_idx + 1 < steps_count:
            down_proj = select_span(adapter_down, span_id)
            up_proj = select_span(adapter_up, span_id)
            pre_act = jnp.einsum(
                "td,rd->tr", current, down_proj, preferred_element_type=jnp.float32
            )
            gated = jax.nn.silu(pre_act).astype(jnp.bfloat16)
            mixed = jnp.dot(gated, up_proj, preferred_element_type=jnp.float32)
            result = (current.astype(jnp.float32) + mixed).astype(jnp.bfloat16)
            current = from_behind(result, "section", 1)
    stacked_rows = jnp.concatenate(pieces, axis=0)
    row_total = stacked_rows.shape[0]
    grouped = stacked_rows.reshape(row_total, model_width // block_size, block_size)
    products = jnp.einsum("tki,tkj->kij", grouped, grouped, preferred_element_type=jnp.float32)
    summed = lax.psum_scatter(
        products.reshape(model_width, block_size).astype(jnp.bfloat16),
        "dp",
        scatter_dimension=0,
        tiled=True,
    ).astype(jnp.float32)
    norm_count = steps_count * tok_rows * replicas
    input_factor_new = 0.75 * input_factor + 0.25 * summed[None] / norm_count
    gradient = returning[0]
    rank_size = stashed.shape[2]
    curv_zero = jnp.zeros((rank_size, rank_size), jnp.float32)
    curv_one = jnp.zeros((rank_size, rank_size), jnp.float32)
    steps_zero = jnp.float32(0.0)
    steps_one = jnp.float32(0.0)
    for step_idx in range(steps_count):
        span_id = (section_index + step_idx < section_count).astype(jnp.int32)
        down_proj = select_span(adapter_down, span_id)
        up_proj = select_span(adapter_up, span_id)
        stash_now = stashed[0, step_idx].T
        grad_act = jnp.einsum("td,rd->tr", gradient, up_proj, preferred_element_type=jnp.float32)
        sigmoid_z = jax.nn.sigmoid(stash_now)
        grad_pre = (grad_act * sigmoid_z * (1.0 + stash_now * (1.0 - sigmoid_z))).astype(
            jnp.bfloat16
        )
        outer = jnp.dot(grad_pre.T, grad_pre, preferred_element_type=jnp.float32)
        in_second = span_id.astype(jnp.float32)
        curv_one = curv_one + outer * in_second
        curv_zero = curv_zero + outer * (1.0 - in_second)
        steps_one = steps_one + in_second
        steps_zero = steps_zero + (1.0 - in_second)
        if step_idx + 1 < steps_count:
            branch = jnp.dot(grad_pre, down_proj, preferred_element_type=jnp.float32)
            passed = (gradient.astype(jnp.float32) + branch).astype(jnp.bfloat16)
            gradient = from_behind(passed, "section", -1)
    curv_total = lax.psum(jnp.stack([curv_zero, curv_one]), "dp")
    step_totals = jnp.stack([steps_zero, steps_one])
    tokens_all = tok_rows * replicas
    divisor = (jnp.maximum(step_totals, 1.0) * tokens_all)[:, None, None]
    updated = 0.75 * output_factor[:, 0] + 0.25 * curv_total / divisor
    output_factor_new = jnp.where((step_totals > 0.0)[:, None, None], updated, output_factor[:, 0])[
        :, None
    ]
    return (input_factor_new, output_factor_new)


def solution(mesh):
    in_specs = (
        P("section", "dp", None),
        P("section", "dp", None),
        P(None, "section", None, None),
        P(None, "section", None, None),
        P("section", None, None, "dp"),
        P(None, "dp"),
        P("section", "dp", None),
        P(None, "section", None, None),
    )
    out_specs = (P("section", "dp", None), P(None, "section", None, None))
    return jax.shard_map(shards, mesh=mesh, in_specs=in_specs, out_specs=out_specs, check_vma=False)
```

profile of v0, /device:TPU:0, one launch (start us, length us, event | category | flops | bytes accessed | tf_op | source)
XLA Modules:
  0.0 288.2 jit_solution(17768884522164974128)
XLA Ops:
  7.2 0.0 copy-start
  7.2 0.0 reduce-scatter.2.cloned.1.call-start
  7.2 1.5 copy-done
  8.8 0.0 copy-start.4
  8.8 6.4 %fusion = bf16[128,8192]{1,0:T(8,128)(2,1)} fusion(bf16[1,128,8192]{2,1,0:T(8,128)(2,1)} %param.8, bf16[2,1,64,8192]{3,2,1,0:T(8,128)(2,1)} %param.11, s32[]{:T(128)S(6)} %select_n.53, bf16[2,1,64,8192]{3,2,1,0:T(8,128)(2,1)S(1)} %copy-done), kind=kOutput, calls=%fused_computation.4 | convolution fusion | flops 271622144 | bytes 8389632 | tf_op jit(solution)/shard_map/dot_general | solution.py:49
  15.1 3.0 %collective-permute-start = (bf16[128,8192]{1,0:T(8,128)(2,1)}, bf16[128,8192]{1,0:T(8,128)(2,1)}, u32[]{:S(2)}, u32[]{:S(2)}) collective-permute-start(bf16[128,8192]{1,0:T(8,128)(2,1)} %fusion), channel_id=1, source_target_pairs={{28,0},{0,4},{4,8},{8,12},{12,16},{16,20},{20,24},{24,28},{29,1},{... | collective-permute-start | bytes 6291464 | tf_op jit(solution)/shard_map/ppermute | solution.py:10
  18.1 0.0 copy-done.4
  18.1 0.2 convert_reduce_fusion
  18.3 4.9 %psum.14 = s32[8,8]{1,0:T(8,128)S(1)} all-reduce(s32[8,8]{1,0:T(8,128)S(1)} %convert_reduce_fusion), channel_id=1, replica_groups=mesh['section'=8,'dp'=4] {'dp'}, use_global_device_ids=true, to_apply=%region_1.0 | all-reduce | flops 64 | bytes 512 | tf_op jit(solution)/shard_map/psum | solution.py:30
  23.3 0.1 fusion.58
  23.4 43.7 %collective-permute-done = bf16[128,8192]{1,0:T(8,128)(2,1)} collective-permute-done((bf16[128,8192]{1,0:T(8,128)(2,1)}, bf16[128,8192]{1,0:T(8,128)(2,1)}, u32[]{:S(2)}, u32[]{:S(2)}) %collective-permute-start) | collective-permute-done | bytes 2097184 | tf_op jit(solution)/shard_map/ppermute | solution.py:10
  67.1 6.4 %fusion.1 = bf16[128,8192]{1,0:T(8,128)(2,1)} fusion(bf16[128,8192]{1,0:T(8,128)(2,1)} %collective-permute-done, bf16[2,1,64,8192]{3,2,1,0:T(8,128)(2,1)} %param.11, s32[]{:T(128)S(6)} %select_n.56, bf16[2,1,64,8192]{3,2,1,0:T(8,128)(2,1)S(1)} %copy-done), kind=kOutput, calls=%fused_computation.5 | convolution fusion | flops 271622144 | bytes 8389632 | tf_op jit(solution)/shard_map/dot_general | solution.py:49
  73.4 0.0 collective-permute-start.1
  73.4 2.0 fusion.5
  75.5 2.0 fusion.6
  77.5 45.6 %collective-permute-done.1 = bf16[128,8192]{1,0:T(8,128)(2,1)S(1)} collective-permute-done((bf16[128,8192]{1,0:T(8,128)(2,1)}, bf16[128,8192]{1,0:T(8,128)(2,1)S(1)}, u32[]{:S(2)}, u32[]{:S(2)}) %collective-permute-start.1) | collective-permute-done | bytes 2097184 | tf_op jit(solution)/shard_map/ppermute | solution.py:10
  123.2 0.4 multiply_convert_fusion
  123.6 7.0 %pad_maximum_fusion = bf16[384,8192]{1,0:T(8,128)(2,1)} fusion(bf16[128,8192]{1,0:T(8,128)(2,1)S(1)} %multiply_convert_fusion, bf16[128,8192]{1,0:T(8,128)(2,1)S(1)} %fusion.6, bf16[128,8192]{1,0:T(8,128)(2,1)S(1)} %fusion.5), kind=kLoop, calls=%fused_computation.10 | loop fusion | flops 18874368 | bytes 12582912 | tf_op jit(solution)/shard_map/concatenate | solution.py:52
  130.6 16.0 %convolution_convert_fusion = bf16[8,1024,1024]{2,1,0:T(8,128)(2,1)} fusion(bf16[48,8,8,1024]{3,2,1,0:T(8,128)(2,1)} %bitcast.174), kind=kOutput, calls=%fused_computation | convolution fusion | flops 6450839552 | bytes 23068672 | tf_op jit(solution)/shard_map/tki,tkj->kij/dot_general | solution.py:55
  146.6 0.0 copy-start.2
  146.6 0.0 reduce-scatter.2.cloned.1.call-update
  146.7 0.9 copy-done.2
  147.5 0.0 copy-start.1
  147.5 3.3 %fusion.25 = bf16[128,64]{0,1:T(8,128)(2,1)S(1)} fusion(bf16[1,128,8192]{2,1,0:T(8,128)(2,1)} %param.9, bf16[2,1,64,8192]{3,2,1,0:T(8,128)(2,1)} %param.11, s32[]{:T(128)S(6)} %select_n.57, f32[1,3,64,128]{3,2,1,0:T(8,128)S(1)} %copy-done.2), kind=kOutput, calls=%fused_computation.29 | convolution fusion | flops 134291456 | bytes 3194884 | tf_op jit(solution)/shard_map/td,rd->tr/dot_general | solution.py:75
  150.8 0.0 copy-done.1
  150.8 2.2 fusion.2
  153.0 0.0 collective-permute-start.2
  153.0 45.7 %collective-permute-done.2 = bf16[128,8192]{1,0:T(8,128)(2,1)} collective-permute-done((bf16[128,8192]{1,0:T(8,128)(2,1)}, bf16[128,8192]{1,0:T(8,128)(2,1)}, u32[]{:S(2)}, u32[]{:S(2)}) %collective-permute-start.2) | collective-permute-done | bytes 2097184 | tf_op jit(solution)/shard_map/ppermute | solution.py:10
  198.7 2.7 fusion.30
  201.4 3.7 %add_convert_fusion = bf16[128,8192]{1,0:T(8,128)(2,1)} fusion(bf16[128,8192]{1,0:T(8,128)(2,1)} %collective-permute-done.2, bf16[128,64]{0,1:T(8,128)(2,1)S(1)} %fusion.30, bf16[2,1,64,8192]{3,2,1,0:T(8,128)(2,1)S(1)} %copy-done, s32[]{:T(128)S(6)} %select_n.58), kind=kOutput, calls=%fused_computation.15 | convolution fusion | flops 137363456 | bytes 5259268 | tf_op jit(solution)/shard_map/dot_general | solution.py:87
  205.1 0.0 copy-start.3
  205.1 3.0 %collective-permute-start.3 = (bf16[128,8192]{1,0:T(8,128)(2,1)}, bf16[128,8192]{1,0:T(8,128)(2,1)}, u32[]{:S(2)}, u32[]{:S(2)}) collective-permute-start(bf16[128,8192]{1,0:T(8,128)(2,1)} %add_convert_fusion), channel_id=1, source_target_pairs={{4,0},{8,4},{12,8},{16,12},{20,16},{24,20},{28,24},{0,28},{5,1},{9... | collective-permute-start | bytes 6291464 | tf_op jit(solution)/shard_map/ppermute | solution.py:10
  208.1 0.1 broadcast_compare_fusion
  208.2 0.1 maximum_multiply_fusion
  208.2 0.1 fusion.111
  208.4 0.1 fusion.112
  208.5 42.2 %collective-permute-done.3 = bf16[128,8192]{1,0:T(8,128)(2,1)} collective-permute-done((bf16[128,8192]{1,0:T(8,128)(2,1)}, bf16[128,8192]{1,0:T(8,128)(2,1)}, u32[]{:S(2)}, u32[]{:S(2)}) %collective-permute-start.3) | collective-permute-done | bytes 2097184 | tf_op jit(solution)/shard_map/ppermute | solution.py:10
  250.7 4.5 %add_bitcast_fusion.1 = (f32[1,64,64]{2,1,0:T(8,128)S(1)}, f32[1,64,64]{2,1,0:T(8,128)S(1)}) fusion(f32[64,64]{1,0:T(8,128)S(1)} %fusion.112, f32[64,64]{1,0:T(8,128)S(1)} %fusion.111, f32[]{:T(128)S(6)} %sub.31, f32[]{:T(128)S(6)} %sub.30, f32[]{:T(128)S(6)} %sub.29, f32[]{:T(128)S(6)} %convert_element_type.126, f32[]{:T(128)S(6)} %convert_element_type.124, ...), kind=kOutput, calls=%fused_computation.81 | convolution fusion | flops 135380992 | bytes 3276828 | tf_op jit(solution)/shard_map/dot_general | solution.py:80
  255.2 12.6 %psum.15 = f32[2,64,64]{2,1,0:T(8,128)S(1)} all-reduce(f32[2,64,64]{2,1,0:T(8,128)S(1)} %pad_maximum_fusion.1), channel_id=1, replica_groups=mesh['section'=8,'dp'=4] {'dp'}, use_global_device_ids=true, to_apply=%region_4.5 | all-reduce | flops 8192 | bytes 65536 | tf_op jit(solution)/shard_map/psum | solution.py:90
  267.8 0.0 copy-done.3
  267.8 0.7 fusion.56
  268.5 2.5 reduce-scatter.2.cloned.1.call-done
  271.0 10.3 %bitcast_add_fusion = f32[1,2048,1024]{2,1,0:T(8,128)} fusion(bf16[2048,1024]{1,0:T(8,128)(2,1)} %reduce-scatter.2.cloned.1.call-done, f32[1,2048,1024]{2,1,0:T(8,128)} %param.14), kind=kLoop, calls=%fused_computation.7 | loop fusion | flops 8388608 | bytes 20971520 | tf_op jit(solution)/shard_map/add | solution.py:63
  (4 shorter events, 0.0 us)
Async XLA Ops:
  7.2 1.6 copy-start
  7.2 263.8 %reduce-scatter.2.cloned.1.call-start = ((), (), s32[]{:S(2)}) async-start(), calls=%async_computation.1 | async-start | bytes 20971520 | tf_op jit(solution)/shard_map/reduce_scatter | solution.py:56
  8.8 9.3 %copy-start.4 = (s32[8,128]{1,0:T(8,128)S(1)}, s32[8,128]{1,0:T(8,128)}, u32[]{:S(2)}) copy-start(s32[8,128]{1,0:T(8,128)} %param.13) | copy-start | bytes 12292
  15.1 52.0 %collective-permute-start = (bf16[128,8192]{1,0:T(8,128)(2,1)}, bf16[128,8192]{1,0:T(8,128)(2,1)}, u32[]{:S(2)}, u32[]{:S(2)}) collective-permute-start(bf16[128,8192]{1,0:T(8,128)(2,1)} %fusion), channel_id=1, source_target_pairs={{28,0},{0,4},{4,8},{8,12},{12,16},{16,20},{20,24},{24,28},{29,1},{... | collective-permute-start | bytes 6291464 | tf_op jit(solution)/shard_map/ppermute | solution.py:10
  73.4 49.7 %collective-permute-start.1 = (bf16[128,8192]{1,0:T(8,128)(2,1)}, bf16[128,8192]{1,0:T(8,128)(2,1)S(1)}, u32[]{:S(2)}, u32[]{:S(2)}) collective-permute-start(bf16[128,8192]{1,0:T(8,128)(2,1)} %fusion.1), channel_id=1, source_target_pairs={{28,0},{0,4},{4,8},{8,12},{12,16},{16,20},{20,24},{24,28},{29,1},{... | collective-permute-start | bytes 6291464 | tf_op jit(solution)/shard_map/ppermute | solution.py:10
  146.6 0.9 copy-start.2
  147.5 3.3 %copy-start.1 = (bf16[1,128,8192]{2,1,0:T(8,128)(2,1)S(1)}, bf16[1,128,8192]{2,1,0:T(8,128)(2,1)}, u32[]{:S(2)}) copy-start(bf16[1,128,8192]{2,1,0:T(8,128)(2,1)} %param.9) | copy-start | bytes 6291460
  153.0 45.7 %collective-permute-start.2 = (bf16[128,8192]{1,0:T(8,128)(2,1)}, bf16[128,8192]{1,0:T(8,128)(2,1)}, u32[]{:S(2)}, u32[]{:S(2)}) collective-permute-start(bf16[128,8192]{1,0:T(8,128)(2,1)} %fusion.2), channel_id=1, source_target_pairs={{4,0},{8,4},{12,8},{16,12},{20,16},{24,20},{28,24},{0,28},{5,1},{9... | collective-permute-start | bytes 6291464 | tf_op jit(solution)/shard_map/ppermute | solution.py:10
  205.1 62.6 %copy-start.3 = (f32[2,1,64,64]{3,2,1,0:T(8,128)S(1)}, f32[2,1,64,64]{3,2,1,0:T(8,128)}, u32[]{:S(2)}) copy-start(f32[2,1,64,64]{3,2,1,0:T(8,128)} %param.15) | copy-start | bytes 98308
  205.1 45.5 %collective-permute-start.3 = (bf16[128,8192]{1,0:T(8,128)(2,1)}, bf16[128,8192]{1,0:T(8,128)(2,1)}, u32[]{:S(2)}, u32[]{:S(2)}) collective-permute-start(bf16[128,8192]{1,0:T(8,128)(2,1)} %add_convert_fusion), channel_id=1, source_target_pairs={{4,0},{8,4},{12,8},{16,12},{20,16},{24,20},{28,24},{0,28},{5,1},{9... | collective-permute-start | bytes 6291464 | tf_op jit(solution)/shard_map/ppermute | solution.py:10
Sparse Core Ops, SparseCore 0:
  146.8 124.2 reduce-scatter.1
where the time goes:
time: 288 us
  waiting for transfers between devices  180 us (62%)
  matrix products  45.3 us (16%)
  other arithmetic  23 us (8%)
  blocking collectives  17.5 us (6%)
  between operations  14.2 us (5%)
  starting transfers between devices  5.96 us (2%)
    ppermute x4, waiting for transfers between devices, from_behind(): return lax.ppermute(block, axis, route)  177 us
    dot_general x1, matrix products, shards(): jnp.einsum('tki,tkj->kij', grouped, grouped, preferred_element_type=jnp.f...  16 us
    dot_general x2, matrix products, shards(): mixed = jnp.dot(gated, up_proj, preferred_element_type=jnp.float32)  12.7 us
    psum x1, blocking collectives, shards(): curv_total = lax.psum(jnp.stack([curv_zero, curv_one]), 'dp')  12.6 us
    add x1, other arithmetic, shards(): input_factor_new = 0.75 * input_factor + 0.25 * summed[None] / norm_count  10.3 us
    concatenate x1, other arithmetic, shards(): stacked_rows = jnp.concatenate(pieces, axis=0)  6.99 us
    dot_general x2, matrix products, shards(): jnp.einsum('td,rd->tr', gradient, up_proj, preferred_element_type=jnp.flo...  5.97 us
    ppermute x4, starting transfers between devices, from_behind(): return lax.ppermute(block, axis, route)  5.92 us
  transfers between devices with their start and end apart: 5, of which 5 were waited for; matrix products, arithmetic and copies ran while one was open for 8% of the time, Pallas kernels for 0%

commit v1 on v0

v1 whole, which is shorter than its diff:
```python
import functools

import jax
import jax.numpy as jnp
from jax import lax
from jax.experimental import pallas as pl
from jax.experimental.pallas import tpu as pltpu
from jax.sharding import PartitionSpec as P

BF16 = jnp.bfloat16
F32 = jnp.float32
ACROSS = (((1,), (1,)), ((), ()))
DOWNWARD = (((0,), (0,)), ((), ()))


def dot_nt(a, b):
    return lax.dot_general(a, b, ACROSS, preferred_element_type=F32)


def dot_nn(a, b):
    return jnp.dot(a, b, preferred_element_type=F32)


def long_dot(a_ref, b_ref, tile):
    width = a_ref.shape[-1]
    total = dot_nt(a_ref[:, 0:tile], b_ref[:, 0:tile])
    for at in range(tile, width, tile):
        total = total + dot_nt(a_ref[:, at : at + tile], b_ref[:, at : at + tile])
    return total


def split_dot_left(wide, narrow):
    high = wide.astype(BF16)
    low = (wide - high.astype(F32)).astype(BF16)
    return dot_nn(high, narrow) + dot_nn(low, narrow)


def split_dot_right(narrow, wide):
    high = wide.astype(BF16)
    low = (wide - high.astype(F32)).astype(BF16)
    return dot_nn(narrow, high) + dot_nn(narrow, low)


def forward_spans(anchor, n):
    first = 1 - anchor // (n // 2)
    return first, first + (anchor + 1) // n


def backward_span(anchor, step, n):
    section = (anchor - step + n) % n
    return 1 - (section + step) // n


def exchange_kernel(
    n, reps, parts,
    ent, ret, down, up, stash, docs,
    buf, upbuf, gbuf, docbuf, cbuf,
    ent_v, ret_v, down_v, up_v, stash_v, wfull, gsrc, msrc, mbuf, csrc,
    local_sem, send_sem, recv_sem,
):
    s = lax.axis_index("section")
    r = lax.axis_index("dp")
    chips = reps // 2
    chip, core = r // 2, r % 2
    tok, width = ent.shape
    rank = up.shape[1]
    share = width // reps
    wide = buf.shape[-1]
    tile = min(2048, width)

    def sec(shift):
        return (s + shift + n) % n

    def rep(dc, e):
        return ((chip + dc + chips) % chips) * 2 + (core + e) % 2

    def cols(replica):
        return pl.ds(pl.multiple_of(replica * share // wide * wide, 128), wide)

    def piece(replica):
        return pl.ds(pl.multiple_of(replica * share, 128), share)

    inner = pl.ds(pl.multiple_of(r * share % wide, 128), share)
    slots = [(d // 2, d % 2) for d in range(reps)]
    counts = {"copy": 0, "local": 0}
    copies = []
    locals_ = []

    def send(src, dst, section, replica):
        at = counts["copy"]
        counts["copy"] += 1
        copy = pltpu.make_async_remote_copy(
            src_ref=src, dst_ref=dst, send_sem=send_sem.at[at], recv_sem=recv_sem.at[at],
            device_id=(section, replica), device_id_type=pl.DeviceIdType.MESH,
        )
        copy.start()
        copies.append(copy)
        return copy

    def keep(src, dst):
        at = counts["local"]
        counts["local"] += 1
        copy = pltpu.make_async_copy(src, dst, local_sem.at[at])
        copy.start()
        return copy

    load_ent = keep(ent, ent_v)
    load_down = keep(down, down_v)
    load_up = keep(up, up_v)
    load_ret = keep(ret, ret_v)
    load_stash = keep(stash.at[0], stash_v.at[0])
    own_chunk = keep(ent.at[:, cols(r)], buf.at[0, 0])
    own_up = keep(up.at[:, :, cols(r)], upbuf.at[0])
    own_docs = keep(docs, docbuf.at[0])

    barrier = pltpu.get_barrier_semaphore()
    peers = 0
    for shift in (0, 1, 2, -1, -2):
        for dc, e in slots:
            if shift == 0 and dc == 0 and e == 0:
                continue
            pl.semaphore_signal(
                barrier, inc=1, device_id=(sec(shift), rep(dc, e)),
                device_id_type=pl.DeviceIdType.MESH,
            )
            peers += 1
    pl.semaphore_wait(barrier, peers)

    prev = sec(-1)
    w1_piece = send(
        down.at[forward_spans(prev, n)[1], :, piece(r)], wfull.at[0, :, piece(r)], prev, r
    )
    ups2 = send(up.at[:, :, cols(r)], upbuf.at[2], sec(2), r)
    st1 = send(stash.at[1], stash_v.at[1], sec(1), r)
    st2 = send(stash.at[2], stash_v.at[2], sec(2), r)
    inside = {}
    for dc, e in slots[1:]:
        target = rep(dc, e)
        inside[dc, e] = send(ent.at[:, cols(target)], buf.at[0, dc * 2 + e], s, target)
    doc_copies = [send(docs, docbuf.at[dc * 2 + e], s, rep(dc, e)) for dc, e in slots[1:]]

    half = tok // parts
    bands = [pl.ds(b * half, half) for b in range(parts)]
    ahead = {}

    def send_ahead(d):
        for b in range(parts):
            ahead[d, b] = send(buf.at[0, d, bands[b]], buf.at[2, d, bands[b]], sec(2), r)

    odd = s % 2
    partner = s + 1 - 2 * odd
    across = {}

    def send_across(d, b):
        ahead[d, b].wait_recv()
        across[d, b] = send(
            buf.at[2 * odd, d, bands[b]], buf.at[1, d, bands[b]], partner, r
        )

    own_chunk.wait()
    send_ahead(0)

    c0, _ = forward_spans(s, n)
    load_ent.wait()
    load_down.wait()
    z0 = long_dot(ent_v, down_v.at[c0], tile)
    g0 = (z0 / (1.0 + jnp.exp(-z0))).astype(BF16)
    gsrc[:, 0:rank] = g0

    inside[0, 1].wait_recv()
    send_ahead(1)

    def gather_start(which, own_ref):
        mine = wfull.at[which, :, piece(r)]
        out = {0: send(own_ref, mine, s, rep(0, 1))}
        for dc in range(1, chips):
            out[dc] = send(own_ref, mine, s, rep(dc, 0))
        return out

    def gather_pass(which, out):
        passed = []
        for dc in range(1, chips):
            out[dc].wait_recv()
            theirs = wfull.at[which, :, piece(rep(-dc, 0))]
            passed.append(send(theirs, theirs, s, rep(0, 1)))
        return passed

    def gather_end(out, passed):
        out[0].wait_recv()
        for copy in passed:
            copy.wait_recv()

    w1_piece.wait_recv()
    w1_out = gather_start(0, wfull.at[0, :, piece(r)])

    own_up.wait()
    ups2.wait_recv()
    ups1 = send(upbuf.at[2 * odd], upbuf.at[1], partner, r)
    span2 = backward_span(s, 2, n)
    own3 = keep(upbuf.at[2, span2, :, inner], wfull.at[2, :, piece(r)])
    w3_out = gather_start(2, upbuf.at[2, span2, :, inner])

    send_across_done = 0
    for d in range(2, reps):
        inside[slots[d]].wait_recv()
        send_ahead(d)
        if d == 2:
            w1_pass = gather_pass(0, w1_out)
            for b in range(parts):
                send_across(0, b)
            send_across_done = 1

    ups1.wait_recv()
    span1 = backward_span(s, 1, n)
    own2 = keep(upbuf.at[1, span1, :, inner], wfull.at[1, :, piece(r)])
    w2_out = gather_start(1, upbuf.at[1, span1, :, inner])
    w3_pass = gather_pass(2, w3_out)

    load_up.wait()
    gather_end(w1_out, w1_pass)
    p01 = long_dot(up_v.at[c0], wfull.at[0], tile)
    z1 = long_dot(ent_v, wfull.at[0], tile) + split_dot_right(g0, p01)
    gsrc[:, rank : 2 * rank] = (z1 / (1.0 + jnp.exp(-z1))).astype(BF16)
    g_copies = []
    for shift in (1, 2):
        for dc, e in slots:
            g_copies.append(send(gsrc, gbuf.at[shift - 1, dc * 2 + e], sec(shift), rep(dc, e)))

    after = sec(1)
    late2, late1 = backward_span(after, 2, n), backward_span(after, 1, n)
    keep(upbuf.at[1, late2, :, inner], msrc.at[0]).wait()
    keep(down.at[late1, :, piece(r)], msrc.at[1]).wait()
    mbuf[reps] = dot_nt(msrc[0], msrc[1])
    m_copies = []
    for dc, e in slots:
        m_copies.append(send(mbuf.at[reps], mbuf.at[dc * 2 + e], after, rep(dc, e)))

    for b in range(parts):
        send_across(1, b)
    w2_pass = gather_pass(1, w2_out)

    def gate(q):
        sigma = 1.0 / (1.0 + jnp.exp(-q))
        return sigma * (1.0 + q * (1.0 - sigma))

    load_ret.wait()
    load_stash.wait()
    a0 = long_dot(up_v.at[1], ret_v, tile)
    dz0 = (a0 * gate(stash_v[0])).astype(BF16)
    csrc[0] = dot_nt(dz0, dz0)
    gather_end(w3_out, w3_pass)
    own3.wait()
    n2 = long_dot(wfull.at[2], down_v.at[1], tile)
    a2 = long_dot(wfull.at[2], ret_v, tile) + split_dot_left(n2, dz0)
    gather_end(w2_out, w2_pass)
    own2.wait()
    n1 = long_dot(wfull.at[1], down_v.at[1], tile)
    a1 = long_dot(wfull.at[1], ret_v, tile) + split_dot_left(n1, dz0)
    st1.wait_recv()
    dz1 = (a1 * gate(stash_v[1])).astype(BF16)
    csrc[1] = dot_nt(dz1, dz1)
    for d in range(2, reps - 1):
        for b in range(parts):
            send_across(d, b)
    for copy in m_copies:
        copy.wait_recv()
    n3 = mbuf[0]
    for d in range(1, reps):
        n3 = n3 + mbuf[d]
    a2 = a2 + split_dot_left(n3, dz1)
    st2.wait_recv()
    dz2 = (a2 * gate(stash_v[2])).astype(BF16)
    csrc[2] = dot_nt(dz2, dz2)
    own_c = keep(csrc.at[0], cbuf.at[0, 0])
    c_copies = []
    for step in range(3):
        for dc, e in slots:
            if step == 0 and dc == 0 and e == 0:
                continue
            c_copies.append(
                send(csrc.at[step], cbuf.at[step, dc * 2 + e], sec(-step), rep(dc, e))
            )
    for b in range(parts):
        send_across(reps - 1, b)

    own_docs.wait()
    own_c.wait()
    for copy in doc_copies + g_copies + c_copies:
        copy.wait_recv()
    for copy in across.values():
        copy.wait_recv()
    for copy in copies:
        copy.wait_send()
    assert counts["copy"] <= send_sem.shape[0] and counts["local"] <= local_sem.shape[0]


def exchange(ent, ret, down, up, stash, docs, n, reps, wide, parts):
    tok, width = ent.shape
    rank = up.shape[1]
    slots = 140 if reps <= 4 else 60 * reps
    anywhere = pl.BlockSpec(memory_space=pl.ANY)
    return pl.pallas_call(
        functools.partial(exchange_kernel, n, reps, parts),
        out_shape=(
            jax.ShapeDtypeStruct((3, reps, tok, wide), BF16),
            jax.ShapeDtypeStruct((3, 2, rank, wide), BF16),
            jax.ShapeDtypeStruct((2, reps, tok, 2 * rank), BF16),
            jax.ShapeDtypeStruct((reps,) + docs.shape, jnp.int32),
            jax.ShapeDtypeStruct((3, reps, rank, rank), F32),
        ),
        in_specs=[anywhere] * 6,
        out_specs=(anywhere,) * 5,
        scratch_shapes=[
            pltpu.VMEM((tok, width), BF16),
            pltpu.VMEM((tok, width), BF16),
            pltpu.VMEM((2, rank, width), BF16),
            pltpu.VMEM((2, rank, width), BF16),
            pltpu.VMEM((3, rank, tok), F32),
            pltpu.VMEM((3, rank, width), BF16),
            pltpu.VMEM((tok, 2 * rank), BF16),
            pltpu.VMEM((2, rank, width // reps), BF16),
            pltpu.VMEM((reps + 1, rank, rank), F32),
            pltpu.VMEM((3, rank, rank), F32),
            pltpu.SemaphoreType.DMA((16,)),
            pltpu.SemaphoreType.DMA((slots,)),
            pltpu.SemaphoreType.DMA((slots,)),
        ],
        compiler_params=pltpu.CompilerParams(
            collective_id=0, has_side_effects=True, vmem_limit_bytes=40 * 1024 * 1024
        ),
        name="exchange",
    )(ent, ret, down, up, stash, docs)


def factor_kernel(n, reps, scale, buf, upbuf, gbuf, weight, old, new, rows):
    s = lax.axis_index("section")
    r = lax.axis_index("dp")
    step = pl.program_id(0)
    _, tokens, wide = buf.shape
    rank = upbuf.shape[2]
    height, block = old.shape
    share = height * pl.num_programs(0)

    @pl.when(step == 0)
    def _():
        piece = min(512, wide)
        back1, back2 = (s - 1 + n) % n, (s - 2 + n) % n
        first1, _ = forward_spans(back1, n)
        first2, second2 = forward_spans(back2, n)

        def fill(at, carry):
            here = pl.ds(pl.multiple_of(at * piece, piece), piece)
            rows[0:tokens, here] = (weight[0] * buf[0, :, here].astype(F32)).astype(BF16)
            act = buf[1, :, here].astype(F32) + dot_nn(
                gbuf[0, :, 0:rank], upbuf[1, first1, :, here]
            )
            act = act.astype(BF16).astype(F32)
            rows[tokens : 2 * tokens, here] = (weight[1] * act).astype(BF16)
            act = buf[2, :, here].astype(F32) + dot_nn(
                gbuf[1, :, 0:rank], upbuf[2, first2, :, here]
            )
            act = act.astype(BF16).astype(F32) + dot_nn(
                gbuf[1, :, rank : 2 * rank], upbuf[1, second2, :, here]
            )
            act = act.astype(BF16).astype(F32)
            rows[2 * tokens : 3 * tokens, here] = (weight[2] * act).astype(BF16)
            return carry

        lax.fori_loop(0, wide // piece, fill, 0)

    width = share * reps
    inside = (r * (width // reps)) % wide if width // reps < wide else 0
    left = pl.multiple_of(inside + step * height, 128)
    right = pl.multiple_of(left // block * block, block)
    total = lax.dot_general(
        rows[:, pl.ds(left, height)], rows[:, pl.ds(right, block)], DOWNWARD,
        preferred_element_type=F32,
    )
    new[...] = 0.75 * old[...] + total * scale


def update_factor(buf, upbuf, gbuf, weight, old, n, reps):
    share, block = old.shape
    _, tokens, wide = buf.shape
    height = min(256, share)
    whole = pl.BlockSpec(memory_space=pltpu.VMEM)
    tile = pl.BlockSpec((height, block), lambda i: (i, 0))
    return pl.pallas_call(
        functools.partial(factor_kernel, n, reps, 0.25 / (3 * tokens)),
        out_shape=jax.ShapeDtypeStruct(old.shape, F32),
        grid=(share // height,),
        in_specs=[whole, whole, whole, whole, tile],
        out_specs=tile,
        scratch_shapes=[pltpu.VMEM((3 * tokens, wide), BF16)],
        compiler_params=pltpu.CompilerParams(vmem_limit_bytes=56 * 1024 * 1024),
        name="factor",
    )(buf, upbuf, gbuf, weight, old)


def shards(
    entering, returning, adapter_down, adapter_up, stashed, doc_ids, input_factor, output_factor
):
    s = lax.axis_index("section")
    n = lax.axis_size("section")
    reps = lax.axis_size("dp")
    tok, width = entering.shape[1:]
    block = input_factor.shape[2]
    steps = stashed.shape[1]
    rank = stashed.shape[2]
    tokens = tok * reps
    wide = max(block, width // reps)
    buf, upbuf, gbuf, docbuf, cbuf = exchange(
        entering[0], returning[0], adapter_down[:, 0], adapter_up[:, 0], stashed[0], doc_ids,
        n, reps, wide, 2,
    )
    anchors = (s - jnp.arange(steps, dtype=jnp.int32)) % n
    mine = jnp.take(docbuf, anchors, axis=1).transpose(1, 0, 2).reshape(steps, tokens)
    same = mine[:, :, None] == jnp.arange(2 * reps, dtype=jnp.int32)
    counts = jnp.sum(same.astype(F32), axis=1)
    length = jnp.sum(jnp.where(same, counts[:, None, :], 0.0), axis=2)
    weight = jnp.sqrt(jnp.sqrt(tok / length))[:, :, None]
    factor = update_factor(
        buf.reshape(steps, tokens, wide), upbuf, gbuf.reshape(2, tokens, 2 * rank), weight,
        input_factor[0], n, reps,
    )
    curv = jnp.sum(cbuf, axis=1)
    second = (s + jnp.arange(steps) < n).astype(F32)
    member = jnp.stack([1.0 - second, second])
    held = jnp.sum(member, axis=1)
    total = jnp.sum(member[:, :, None, None] * curv[None], axis=1)
    divisor = (jnp.maximum(held, 1.0) * tokens)[:, None, None]
    updated = 0.75 * output_factor[:, 0] + 0.25 * total / divisor
    outer = jnp.where((held > 0.0)[:, None, None], updated, output_factor[:, 0])
    return factor[None], outer[:, None]


def solution(mesh):
    in_specs = (
        P("section", "dp", None),
        P("section", "dp", None),
        P(None, "section", None, None),
        P(None, "section", None, None),
        P("section", None, None, "dp"),
        P(None, "dp"),
        P("section", "dp", None),
        P(None, "section", None, None),
    )
    out_specs = (P("section", "dp", None), P(None, "section", None, None))
    return jax.shard_map(shards, mesh=mesh, in_specs=in_specs, out_specs=out_specs, check_vma=False)
```

time: 288 us -> 127 us (0.44)
  waiting for transfers between devices: 180 us -> 0 us
  Pallas kernels: 0 us -> 113 us
  matrix products: 45.3 us -> 0 us
  other arithmetic: 23 us -> 1.22 us
  blocking collectives: 17.5 us -> 0 us
  between operations: 14.2 us -> 0.73 us
  local copies, waits for them, and re-layouts: 2.43 us -> 11.6 us
  starting transfers between devices: 5.96 us -> 0 us
    ppermute x4 -> x0, waiting for transfers between devices: 177 us -> none  [from_behind(): return lax.ppermute(block, axis, route)]
    pallas_call x0 -> x2, Pallas kernels: none -> 113 us  [the longest x1 95 us: exchange(): pl.pallas_call(functools.partial(exchange_kernel, n, reps, parts), out_sh...]
    dot_general x10 -> x0, matrix products: 45.3 us -> none  [the longest x1 16 us: shards(): jnp.einsum('tki,tkj->kij', grouped, grouped, preferred_element_type=jnp.f...]
    psum x2 -> x0, blocking collectives: 17.5 us -> none  [the longest x1 12.6 us: shards(): curv_total = lax.psum(jnp.stack([curv_zero, curv_one]), 'dp')]
    add x1 -> x0, other arithmetic: 10.3 us -> none  [shards(): input_factor_new = 0.75 * input_factor + 0.25 * summed[None] / norm_count]
    unnamed x10 -> x19, local copies, waits for them, and re-layouts: 2.41 us -> 9.79 us
    concatenate x1 -> x0, other arithmetic: 6.99 us -> none  [shards(): stacked_rows = jnp.concatenate(pieces, axis=0)]
    ppermute x4 -> x0, starting transfers between devices: 5.92 us -> none  [from_behind(): return lax.ppermute(block, axis, route)]
  transfers between devices with their start and end apart: 5 -> 0, of which waited for: 5 -> 0; matrix products, arithmetic and copies ran while one was open for 8% -> 0% of each run, Pallas kernels for 0% -> 0%
where the time goes in v1:
time: 127 us; the launch traced here: 126 us
  Pallas kernels  113 us (89%)
  local copies, waits for them, and re-layouts  11.6 us (9%)
    pallas_call x1, Pallas kernels, exchange(): pl.pallas_call(functools.partial(exchange_kernel, n, reps, parts), out_sh...  95 us
    pallas_call x1, Pallas kernels, update_factor(): pl.pallas_call(functools.partial(factor_kernel, n, reps, 0.25 / (3 * toke...  17.7 us
    unnamed x19, local copies, waits for them, and re-layouts  9.79 us

profile of v1, /device:TPU:0, one launch (start us, length us, event | category | flops | bytes accessed | tf_op | source)
XLA Modules:
  0.0 126.3 jit_solution(3100185480863272357)
XLA Ops:
  0.7 0.1 fusion.10
  0.8 0.0 copy-start
  0.9 1.6 %copy-done = bf16[1,128,8192]{2,1,0:T(8,128)(2,1)S(1)} copy-done((bf16[1,128,8192]{2,1,0:T(8,128)(2,1)S(1)}, bf16[1,128,8192]{2,1,0:T(8,128)(2,1)}, u32[]{:S(2)}) %copy-start) | copy-done | bytes 2097176
  2.4 0.0 copy-start.1
  2.4 1.6 %copy-done.1 = bf16[1,128,8192]{2,1,0:T(8,128)(2,1)S(1)} copy-done((bf16[1,128,8192]{2,1,0:T(8,128)(2,1)S(1)}, bf16[1,128,8192]{2,1,0:T(8,128)(2,1)}, u32[]{:S(2)}) %copy-start.1) | copy-done | bytes 2097176
  4.0 0.0 copy-start.2
  4.0 1.6 %copy-done.2 = bf16[2,1,64,8192]{3,2,1,0:T(8,128)(2,1)S(1)} copy-done((bf16[2,1,64,8192]{3,2,1,0:T(8,128)(2,1)S(1)}, bf16[2,1,64,8192]{3,2,1,0:T(8,128)(2,1)}, u32[]{:S(2)}) %copy-start.2) | copy-done | bytes 2097176
  5.6 0.0 copy-start.3
  5.6 1.6 %copy-done.3 = bf16[2,1,64,8192]{3,2,1,0:T(8,128)(2,1)S(1)} copy-done((bf16[2,1,64,8192]{3,2,1,0:T(8,128)(2,1)S(1)}, bf16[2,1,64,8192]{3,2,1,0:T(8,128)(2,1)}, u32[]{:S(2)}) %copy-start.3) | copy-done | bytes 2097176
  7.2 0.0 copy-start.6
  7.2 0.9 copy-done.6
  8.1 0.0 copy-start.7
  8.1 0.7 copy-done.7
  8.8 0.0 copy-start.8
  8.8 95.0 %exchange.1 = (bf16[3,4,128,2048]{3,2,1,0:T(8,128)(2,1)}, bf16[3,2,64,2048]{3,2,1,0:T(8,128)(2,1)S(1)}, bf16[2,4,128,128]{3,2,1,0:T(8,128)(2,1)S(1)}, s32[4,8,128]{2,1,0:T(8,128)S(1)}, f32[3,4,64,64]{3,2,1,0:T(8,128)S(1)}) custom-call(bf16[128,8192]{1,0:T(8,128)(2,1)S(1)} %bitcast.33, bf16[128,8192]{1,0:T(8,128)(2,1)S(1)} %bitcast.34, ...), custom_call_target="tpu_custom_call" | custom-call | tf_op jit(solution)/shard_map/exchange/pallas_call | solution.py:302
  103.8 0.0 copy-start.4
  103.9 1.1 copy-done.4
  105.0 0.0 copy-start.5
  105.0 0.7 copy-done.5
  105.7 0.6 gather_fusion
  106.3 0.1 select_bitcast_fusion
  106.3 0.1 fusion.11
  106.5 0.1 multiply_reduce_fusion
  106.6 0.0 copy-done.8
  106.6 0.7 fusion.5
  107.4 1.2 copy.13.weight
  108.6 17.7 %factor.1 = f32[2048,1024]{1,0:T(8,128)} custom-call(bf16[3,512,2048]{2,1,0:T(8,128)(2,1)} %bitcast.41, bf16[3,2,64,2048]{3,2,1,0:T(8,128)(2,1)} %copy-done.4, bf16[2,512,128]{2,1,0:T(8,128)(2,1)} %bitcast.37, f32[3,512,1]{2,1,0:T(8,128)} %copy.13.weight, f32[2048,1024]{1,0:T(8,128)} %bitcast.39), custom_call_target="tpu_custom_call" | custom-call | tf_op jit(solution)/shard_map/factor/pallas_call | solution.py:388
  (11 shorter events, 0.1 us)
Async XLA Ops:
  0.8 1.6 %copy-start = (bf16[1,128,8192]{2,1,0:T(8,128)(2,1)S(1)}, bf16[1,128,8192]{2,1,0:T(8,128)(2,1)}, u32[]{:S(2)}) copy-start(bf16[1,128,8192]{2,1,0:T(8,128)(2,1)} %param.8) | copy-start | bytes 6291460
  2.4 1.6 %copy-start.1 = (bf16[1,128,8192]{2,1,0:T(8,128)(2,1)S(1)}, bf16[1,128,8192]{2,1,0:T(8,128)(2,1)}, u32[]{:S(2)}) copy-start(bf16[1,128,8192]{2,1,0:T(8,128)(2,1)} %param.9) | copy-start | bytes 6291460
  4.0 1.6 %copy-start.2 = (bf16[2,1,64,8192]{3,2,1,0:T(8,128)(2,1)S(1)}, bf16[2,1,64,8192]{3,2,1,0:T(8,128)(2,1)}, u32[]{:S(2)}) copy-start(bf16[2,1,64,8192]{3,2,1,0:T(8,128)(2,1)} %param.10) | copy-start | bytes 6291460
  5.6 1.6 %copy-start.3 = (bf16[2,1,64,8192]{3,2,1,0:T(8,128)(2,1)S(1)}, bf16[2,1,64,8192]{3,2,1,0:T(8,128)(2,1)}, u32[]{:S(2)}) copy-start(bf16[2,1,64,8192]{3,2,1,0:T(8,128)(2,1)} %param.11) | copy-start | bytes 6291460
  7.2 0.9 copy-start.6
  8.1 0.7 copy-start.7
  8.8 97.8 %copy-start.8 = (f32[2,1,64,64]{3,2,1,0:T(8,128)S(1)}, f32[2,1,64,64]{3,2,1,0:T(8,128)}, u32[]{:S(2)}) copy-start(f32[2,1,64,64]{3,2,1,0:T(8,128)} %param.15) | copy-start | bytes 98308
  103.8 1.1 copy-start.4
  105.0 0.7 copy-start.5

commit v2 on v1

--- a/solution.py
+++ b/solution.py
@@ -126,49 +126,50 @@
             peers += 1
     pl.semaphore_wait(barrier, peers)
 
+    half = tok // parts
+    bands = [pl.ds(b * half, half) for b in range(parts)]
+    pieces = [("e", 0, b) for b in range(parts)] + [("u", 0, 0), ("u", 1, 0)]
+    pieces += [("e", d, b) for d in range(1, reps) for b in range(parts)]
+    inside, ahead, across = {}, {}, {}
+    arrived = set()
+    odd = s % 2
+    partner = s + 1 - 2 * odd
+
+    def send_ahead(at):
+        kind, d, b = pieces[at]
+        if kind == "u":
+            src, dst = up.at[d, :, cols(r)], upbuf.at[2, d]
+        else:
+            dst = buf.at[2, d, bands[b]]
+            if d == 0:
+                src = ent.at[bands[b], cols(r)]
+            else:
+                src = buf.at[0, d, bands[b]]
+                if d not in arrived:
+                    inside[slots[d]].wait_recv()
+                    arrived.add(d)
+        ahead[at] = send(src, dst, sec(2), r)
+
+    def send_across(at):
+        kind, d, b = pieces[at]
+        if kind == "u":
+            src, dst = upbuf.at[2 * odd, d], upbuf.at[1, d]
+        else:
+            src, dst = buf.at[2 * odd, d, bands[b]], buf.at[1, d, bands[b]]
+        across[kind, d, b] = send(src, dst, partner, r)
+
+    send_ahead(0)
+    send_ahead(1)
     prev = sec(-1)
     w1_piece = send(
         down.at[forward_spans(prev, n)[1], :, piece(r)], wfull.at[0, :, piece(r)], prev, r
     )
-    ups2 = send(up.at[:, :, cols(r)], upbuf.at[2], sec(2), r)
-    st1 = send(stash.at[1], stash_v.at[1], sec(1), r)
-    st2 = send(stash.at[2], stash_v.at[2], sec(2), r)
-    inside = {}
     for dc, e in slots[1:]:
         target = rep(dc, e)
         inside[dc, e] = send(ent.at[:, cols(target)], buf.at[0, dc * 2 + e], s, target)
     doc_copies = [send(docs, docbuf.at[dc * 2 + e], s, rep(dc, e)) for dc, e in slots[1:]]
-
-    half = tok // parts
-    bands = [pl.ds(b * half, half) for b in range(parts)]
-    ahead = {}
-
-    def send_ahead(d):
-        for b in range(parts):
-            ahead[d, b] = send(buf.at[0, d, bands[b]], buf.at[2, d, bands[b]], sec(2), r)
-
-    odd = s % 2
-    partner = s + 1 - 2 * odd
-    across = {}
-
-    def send_across(d, b):
-        ahead[d, b].wait_recv()
-        across[d, b] = send(
-            buf.at[2 * odd, d, bands[b]], buf.at[1, d, bands[b]], partner, r
-        )
-
-    own_chunk.wait()
-    send_ahead(0)
-
-    c0, _ = forward_spans(s, n)
-    load_ent.wait()
-    load_down.wait()
-    z0 = long_dot(ent_v, down_v.at[c0], tile)
-    g0 = (z0 / (1.0 + jnp.exp(-z0))).astype(BF16)
-    gsrc[:, 0:rank] = g0
-
-    inside[0, 1].wait_recv()
-    send_ahead(1)
+    st1 = send(stash.at[1], stash_v.at[1], sec(1), r)
+    st2 = send(stash.at[2], stash_v.at[2], sec(2), r)
 
     def gather_start(which, own_ref):
         mine = wfull.at[which, :, piece(r)]
@@ -190,105 +191,123 @@
         for copy in passed:
             copy.wait_recv()
 
-    w1_piece.wait_recv()
-    w1_out = gather_start(0, wfull.at[0, :, piece(r)])
-
-    own_up.wait()
-    ups2.wait_recv()
-    ups1 = send(upbuf.at[2 * odd], upbuf.at[1], partner, r)
-    span2 = backward_span(s, 2, n)
-    own3 = keep(upbuf.at[2, span2, :, inner], wfull.at[2, :, piece(r)])
-    w3_out = gather_start(2, upbuf.at[2, span2, :, inner])
-
-    send_across_done = 0
-    for d in range(2, reps):
-        inside[slots[d]].wait_recv()
-        send_ahead(d)
-        if d == 2:
-            w1_pass = gather_pass(0, w1_out)
-            for b in range(parts):
-                send_across(0, b)
-            send_across_done = 1
-
-    ups1.wait_recv()
-    span1 = backward_span(s, 1, n)
-    own2 = keep(upbuf.at[1, span1, :, inner], wfull.at[1, :, piece(r)])
-    w2_out = gather_start(1, upbuf.at[1, span1, :, inner])
-    w3_pass = gather_pass(2, w3_out)
-
-    load_up.wait()
-    gather_end(w1_out, w1_pass)
-    p01 = long_dot(up_v.at[c0], wfull.at[0], tile)
-    z1 = long_dot(ent_v, wfull.at[0], tile) + split_dot_right(g0, p01)
-    gsrc[:, rank : 2 * rank] = (z1 / (1.0 + jnp.exp(-z1))).astype(BF16)
-    g_copies = []
-    for shift in (1, 2):
-        for dc, e in slots:
-            g_copies.append(send(gsrc, gbuf.at[shift - 1, dc * 2 + e], sec(shift), rep(dc, e)))
-
-    after = sec(1)
-    late2, late1 = backward_span(after, 2, n), backward_span(after, 1, n)
-    keep(upbuf.at[1, late2, :, inner], msrc.at[0]).wait()
-    keep(down.at[late1, :, piece(r)], msrc.at[1]).wait()
-    mbuf[reps] = dot_nt(msrc[0], msrc[1])
-    m_copies = []
-    for dc, e in slots:
-        m_copies.append(send(mbuf.at[reps], mbuf.at[dc * 2 + e], after, rep(dc, e)))
-
-    for b in range(parts):
-        send_across(1, b)
-    w2_pass = gather_pass(1, w2_out)
-
     def gate(q):
         sigma = 1.0 / (1.0 + jnp.exp(-q))
         return sigma * (1.0 + q * (1.0 - sigma))
 
-    load_ret.wait()
-    load_stash.wait()
-    a0 = long_dot(up_v.at[1], ret_v, tile)
-    dz0 = (a0 * gate(stash_v[0])).astype(BF16)
-    csrc[0] = dot_nt(dz0, dz0)
-    gather_end(w3_out, w3_pass)
-    own3.wait()
-    n2 = long_dot(wfull.at[2], down_v.at[1], tile)
-    a2 = long_dot(wfull.at[2], ret_v, tile) + split_dot_left(n2, dz0)
-    gather_end(w2_out, w2_pass)
-    own2.wait()
-    n1 = long_dot(wfull.at[1], down_v.at[1], tile)
-    a1 = long_dot(wfull.at[1], ret_v, tile) + split_dot_left(n1, dz0)
-    st1.wait_recv()
-    dz1 = (a1 * gate(stash_v[1])).astype(BF16)
-    csrc[1] = dot_nt(dz1, dz1)
-    for d in range(2, reps - 1):
-        for b in range(parts):
-            send_across(d, b)
-    for copy in m_copies:
-        copy.wait_recv()
-    n3 = mbuf[0]
-    for d in range(1, reps):
-        n3 = n3 + mbuf[d]
-    a2 = a2 + split_dot_left(n3, dz1)
-    st2.wait_recv()
-    dz2 = (a2 * gate(stash_v[2])).astype(BF16)
-    csrc[2] = dot_nt(dz2, dz2)
-    own_c = keep(csrc.at[0], cbuf.at[0, 0])
-    c_copies = []
-    for step in range(3):
+    held = {}
+    g_copies, m_copies, c_copies = [], [], []
+    c0, _ = forward_spans(s, n)
+    span1, span2 = backward_span(s, 1, n), backward_span(s, 2, n)
+    after = sec(1)
+
+    load_ent.wait()
+    load_down.wait()
+    z0 = long_dot(ent_v, down_v.at[c0], tile)
+    g0 = (z0 / (1.0 + jnp.exp(-z0))).astype(BF16)
+    gsrc[:, 0:rank] = g0
+
+    def work0():
+        own_chunk.wait()
+        own_up.wait()
+        w1_piece.wait_recv()
+        held["w1"] = gather_start(0, wfull.at[0, :, piece(r)])
+
+    def work1():
+        load_up.wait()
+        load_ret.wait()
+        load_stash.wait()
+        a0 = long_dot(up_v.at[1], ret_v, tile)
+        dz0 = (a0 * gate(stash_v[0])).astype(BF16)
+        csrc[0] = dot_nt(dz0, dz0)
+        held["dz0"] = dz0
+
+    def work2():
+        held["w1p"] = gather_pass(0, held["w1"])
+
+    def work3():
+        held["own3"] = keep(upbuf.at[2, span2, :, inner], wfull.at[2, :, piece(r)])
+        held["w3"] = gather_start(2, upbuf.at[2, span2, :, inner])
+        gather_end(held["w1"], held["w1p"])
+        p01 = long_dot(up_v.at[c0], wfull.at[0], tile)
+        z1 = long_dot(ent_v, wfull.at[0], tile) + split_dot_right(g0, p01)
+        gsrc[:, rank : 2 * rank] = (z1 / (1.0 + jnp.exp(-z1))).astype(BF16)
+        for shift in (1, 2):
+            for dc, e in slots:
+                g_copies.append(
+                    send(gsrc, gbuf.at[shift - 1, dc * 2 + e], sec(shift), rep(dc, e))
+                )
+
+    def work4():
+        held["w3p"] = gather_pass(2, held["w3"])
+
+    def work5():
+        across["u", 0, 0].wait_recv()
+        across["u", 1, 0].wait_recv()
+        held["own2"] = keep(upbuf.at[1, span1, :, inner], wfull.at[1, :, piece(r)])
+        held["w2"] = gather_start(1, upbuf.at[1, span1, :, inner])
+        late2, late1 = backward_span(after, 2, n), backward_span(after, 1, n)
+        first = keep(upbuf.at[1, late2, :, inner], msrc.at[0])
+        second = keep(down.at[late1, :, piece(r)], msrc.at[1])
+        first.wait()
+        second.wait()
+        mbuf[reps] = dot_nt(msrc[0], msrc[1])
         for dc, e in slots:
-            if step == 0 and dc == 0 and e == 0:
-                continue
-            c_copies.append(
-                send(csrc.at[step], cbuf.at[step, dc * 2 + e], sec(-step), rep(dc, e))
-            )
-    for b in range(parts):
-        send_across(reps - 1, b)
+            m_copies.append(send(mbuf.at[reps], mbuf.at[dc * 2 + e], after, rep(dc, e)))
+
+    def work6():
+        held["w2p"] = gather_pass(1, held["w2"])
+        gather_end(held["w3"], held["w3p"])
+        held["own3"].wait()
+        n2 = long_dot(wfull.at[2], down_v.at[1], tile)
+        held["a2"] = long_dot(wfull.at[2], ret_v, tile) + split_dot_left(n2, held["dz0"])
+
+    def work7():
+        gather_end(held["w2"], held["w2p"])
+        held["own2"].wait()
+        n1 = long_dot(wfull.at[1], down_v.at[1], tile)
+        a1 = long_dot(wfull.at[1], ret_v, tile) + split_dot_left(n1, held["dz0"])
+        st1.wait_recv()
+        dz1 = (a1 * gate(stash_v[1])).astype(BF16)
+        csrc[1] = dot_nt(dz1, dz1)
+        for copy in m_copies:
+            copy.wait_recv()
+        n3 = mbuf[0]
+        for d in range(1, reps):
+            n3 = n3 + mbuf[d]
+        a2 = held["a2"] + split_dot_left(n3, dz1)
+        st2.wait_recv()
+        dz2 = (a2 * gate(stash_v[2])).astype(BF16)
+        csrc[2] = dot_nt(dz2, dz2)
+        held["own_c"] = keep(csrc.at[0], cbuf.at[0, 0])
+        for step in range(3):
+            for dc, e in slots:
+                if step == 0 and dc == 0 and e == 0:
+                    continue
+                c_copies.append(
+                    send(csrc.at[step], cbuf.at[step, dc * 2 + e], sec(-step), rep(dc, e))
+                )
+
+    works = [work0, work1, work2, work3, work4, work5, work6, work7]
+    for at in range(len(pieces)):
+        ahead[at].wait_recv()
+        if at + 2 < len(pieces):
+            send_ahead(at + 2)
+        if at == 0:
+            works[0]()
+            send_across(at)
+            continue
+        send_across(at)
+        if at < len(works):
+            works[at]()
 
     own_docs.wait()
-    own_c.wait()
+    held["own_c"].wait()
     for copy in doc_copies + g_copies + c_copies:
         copy.wait_recv()
-    for copy in across.values():
-        copy.wait_recv()
+    for (kind, _, _), copy in across.items():
+        if kind == "e":
+            copy.wait_recv()
     for copy in copies:
         copy.wait_send()
     assert counts["copy"] <= send_sem.shape[0] and counts["local"] <= local_sem.shape[0]
@@ -298,7 +317,7 @@
     tok, width = ent.shape
     rank = up.shape[1]
     slots = 140 if reps <= 4 else 60 * reps
-    anywhere = pl.BlockSpec(memory_space=pl.ANY)
+    anywhere = pl.BlockSpec(memory_space=pltpu.HBM)
     return pl.pallas_call(
         functools.partial(exchange_kernel, n, reps, parts),
         out_shape=(
@@ -326,7 +345,7 @@
             pltpu.SemaphoreType.DMA((slots,)),
         ],
         compiler_params=pltpu.CompilerParams(
-            collective_id=0, has_side_effects=True, vmem_limit_bytes=40 * 1024 * 1024
+            collective_id=0, has_side_effects=True, vmem_limit_bytes=63 * 1024 * 1024
         ),
         name="exchange",
     )(ent, ret, down, up, stash, docs)
@@ -392,7 +411,7 @@
         in_specs=[whole, whole, whole, whole, tile],
         out_specs=tile,
         scratch_shapes=[pltpu.VMEM((3 * tokens, wide), BF16)],
-        compiler_params=pltpu.CompilerParams(vmem_limit_bytes=56 * 1024 * 1024),
+        compiler_params=pltpu.CompilerParams(vmem_limit_bytes=63 * 1024 * 1024),
         name="factor",
     )(buf, upbuf, gbuf, weight, old)
 

time: 127 us -> 128 us (level)
  local copies, waits for them, and re-layouts: 11.6 us -> 2.55 us
  Pallas kernels: 113 us -> 122 us
    unnamed x19 -> x3, local copies, waits for them, and re-layouts: 9.79 us -> 0.01 us
    pallas_call x1, Pallas kernels: 95 us -> 104 us  [exchange(): pl.pallas_call(functools.partial(exchange_kernel, n, reps, parts), out_sh...]
where the time goes in v2:
time: 128 us; the launch traced here: 127 us
  Pallas kernels  122 us (95%)
  local copies, waits for them, and re-layouts  2.55 us (2%)
  other arithmetic  2.23 us (2%)
    pallas_call x1, Pallas kernels, exchange(): pl.pallas_call(functools.partial(exchange_kernel, n, reps, parts), out_sh...  104 us
    pallas_call x1, Pallas kernels, update_factor(): pl.pallas_call(functools.partial(factor_kernel, n, reps, 0.25 / (3 * toke...  17.7 us

profile of v2, /device:TPU:0, one launch (start us, length us, event | category | flops | bytes accessed | tf_op | source)
XLA Modules:
  0.0 127.4 jit_solution(18075782849930631312)
XLA Ops:
  0.7 0.1 fusion.10
  0.8 0.0 copy-start
  0.9 104.2 %exchange.1 = (bf16[3,4,128,2048]{3,2,1,0:T(8,128)(2,1)}, bf16[3,2,64,2048]{3,2,1,0:T(8,128)(2,1)}, bf16[2,4,128,128]{3,2,1,0:T(8,128)(2,1)}, s32[4,8,128]{2,1,0:T(8,128)}, f32[3,4,64,64]{3,2,1,0:T(8,128)}) custom-call(bf16[128,8192]{1,0:T(8,128)(2,1)} %bitcast.36, bf16[128,8192]{1,0:T(8,128)(2,1)} %bitcast.37, bf16[2,64,8192]{2,1,0:T(8,128)(2,1)} %bitcast.38, ...), custom_call_target="tpu_custom_call" | custom-call | tf_op jit(solution)/shard_map/exchange/pallas_call | solution.py:321
  105.1 0.7 copy.12
  105.8 0.6 gather_fusion
  106.4 0.1 select_bitcast_fusion
  106.5 0.1 fusion.11
  106.6 1.0 reduce_sum.48
  107.6 0.1 multiply_reduce_fusion
  107.7 0.0 copy-done
  107.7 0.7 fusion.5
  108.5 1.2 copy.13.weight
  109.7 17.7 %factor.1 = f32[2048,1024]{1,0:T(8,128)} custom-call(bf16[3,512,2048]{2,1,0:T(8,128)(2,1)} %bitcast.35, bf16[3,2,64,2048]{3,2,1,0:T(8,128)(2,1)} %get-tuple-element.8.upbuf, bf16[2,512,128]{2,1,0:T(8,128)(2,1)} %bitcast.40, f32[3,512,1]{2,1,0:T(8,128)} %copy.13.weight, f32[2048,1024]{1,0:T(8,128)} %bitcast.33), custom_call_target="tpu_custom_call" | custom-call | tf_op jit(solution)/shard_map/factor/pallas_call | solution.py:407
  (9 shorter events, 0.1 us)
Async XLA Ops:
  0.8 106.9 %copy-start = (f32[2,1,64,64]{3,2,1,0:T(8,128)S(1)}, f32[2,1,64,64]{3,2,1,0:T(8,128)}, u32[]{:S(2)}) copy-start(f32[2,1,64,64]{3,2,1,0:T(8,128)} %param.15) | copy-start | bytes 98308

commit v3 on v2

--- a/solution.py
+++ b/solution.py
@@ -55,7 +55,7 @@
     n, reps, parts,
     ent, ret, down, up, stash, docs,
     buf, upbuf, gbuf, docbuf, cbuf,
-    ent_v, ret_v, down_v, up_v, stash_v, wfull, gsrc, msrc, mbuf, csrc,
+    fleft, fright, bleft, bright, stash_v, gsrc, msrc, mbuf, csrc,
     local_sem, send_sem, recv_sem,
 ):
     s = lax.axis_index("section")
@@ -104,11 +104,18 @@
         copy.start()
         return copy
 
-    load_ent = keep(ent, ent_v)
-    load_down = keep(down, down_v)
-    load_up = keep(up, up_v)
-    load_ret = keep(ret, ret_v)
-    load_stash = keep(stash.at[0], stash_v.at[0])
+    c0, _ = forward_spans(s, n)
+    forward_loads = [
+        keep(ent, fleft.at[pl.ds(0, tok)]),
+        keep(up.at[c0], fleft.at[pl.ds(tok, rank)]),
+        keep(down.at[c0], fright.at[pl.ds(0, rank)]),
+    ]
+    backward_loads = [
+        keep(ret, bright.at[pl.ds(0, tok)]),
+        keep(down.at[1], bright.at[pl.ds(tok, rank)]),
+        keep(up.at[1], bleft.at[pl.ds(0, rank)]),
+        keep(stash.at[0], stash_v.at[0]),
+    ]
     own_chunk = keep(ent.at[:, cols(r)], buf.at[0, 0])
     own_up = keep(up.at[:, :, cols(r)], upbuf.at[0])
     own_docs = keep(docs, docbuf.at[0])
@@ -130,8 +137,12 @@
     bands = [pl.ds(b * half, half) for b in range(parts)]
     pieces = [("e", 0, b) for b in range(parts)] + [("u", 0, 0), ("u", 1, 0)]
     pieces += [("e", d, b) for d in range(1, reps) for b in range(parts)]
+    fulls = [
+        (fright, pl.ds(rank, rank)), (bleft, pl.ds(rank, rank)), (bleft, pl.ds(2 * rank, rank))
+    ]
     inside, ahead, across = {}, {}, {}
     arrived = set()
+    window = 3
     odd = s % 2
     partner = s + 1 - 2 * odd
 
@@ -158,11 +169,11 @@
             src, dst = buf.at[2 * odd, d, bands[b]], buf.at[1, d, bands[b]]
         across[kind, d, b] = send(src, dst, partner, r)
 
-    send_ahead(0)
-    send_ahead(1)
+    for at in range(window):
+        send_ahead(at)
     prev = sec(-1)
     w1_piece = send(
-        down.at[forward_spans(prev, n)[1], :, piece(r)], wfull.at[0, :, piece(r)], prev, r
+        down.at[forward_spans(prev, n)[1], :, piece(r)], fright.at[pl.ds(rank, rank), piece(r)], prev, r
     )
     for dc, e in slots[1:]:
         target = rep(dc, e)
@@ -172,7 +183,8 @@
     st2 = send(stash.at[2], stash_v.at[2], sec(2), r)
 
     def gather_start(which, own_ref):
-        mine = wfull.at[which, :, piece(r)]
+        full, rows = fulls[which]
+        mine = full.at[rows, piece(r)]
         out = {0: send(own_ref, mine, s, rep(0, 1))}
         for dc in range(1, chips):
             out[dc] = send(own_ref, mine, s, rep(dc, 0))
@@ -182,7 +194,8 @@
         passed = []
         for dc in range(1, chips):
             out[dc].wait_recv()
-            theirs = wfull.at[which, :, piece(rep(-dc, 0))]
+            full, rows = fulls[which]
+            theirs = full.at[rows, piece(rep(-dc, 0))]
             passed.append(send(theirs, theirs, s, rep(0, 1)))
         return passed
 
@@ -197,54 +210,44 @@
 
     held = {}
     g_copies, m_copies, c_copies = [], [], []
-    c0, _ = forward_spans(s, n)
     span1, span2 = backward_span(s, 1, n), backward_span(s, 2, n)
     after = sec(1)
-
-    load_ent.wait()
-    load_down.wait()
-    z0 = long_dot(ent_v, down_v.at[c0], tile)
-    g0 = (z0 / (1.0 + jnp.exp(-z0))).astype(BF16)
-    gsrc[:, 0:rank] = g0
 
     def work0():
         own_chunk.wait()
         own_up.wait()
         w1_piece.wait_recv()
-        held["w1"] = gather_start(0, wfull.at[0, :, piece(r)])
+        held["w1"] = gather_start(0, fright.at[pl.ds(rank, rank), piece(r)])
 
     def work1():
-        load_up.wait()
-        load_ret.wait()
-        load_stash.wait()
-        a0 = long_dot(up_v.at[1], ret_v, tile)
-        dz0 = (a0 * gate(stash_v[0])).astype(BF16)
-        csrc[0] = dot_nt(dz0, dz0)
-        held["dz0"] = dz0
+        for load in forward_loads + backward_loads:
+            load.wait()
 
     def work2():
         held["w1p"] = gather_pass(0, held["w1"])
 
     def work3():
-        held["own3"] = keep(upbuf.at[2, span2, :, inner], wfull.at[2, :, piece(r)])
+        held["own3"] = keep(upbuf.at[2, span2, :, inner], bleft.at[pl.ds(2 * rank, rank), piece(r)])
         held["w3"] = gather_start(2, upbuf.at[2, span2, :, inner])
+    def work4():
+        held["w3p"] = gather_pass(2, held["w3"])
         gather_end(held["w1"], held["w1p"])
-        p01 = long_dot(up_v.at[c0], wfull.at[0], tile)
-        z1 = long_dot(ent_v, wfull.at[0], tile) + split_dot_right(g0, p01)
-        gsrc[:, rank : 2 * rank] = (z1 / (1.0 + jnp.exp(-z1))).astype(BF16)
+        both = long_dot(fleft, fright, tile)
+        z = both[0:tok]
+        g0 = (z / (1.0 + jnp.exp(-z)))[:, 0:rank].astype(BF16)
+        later = lax.broadcasted_iota(jnp.int32, z.shape, 1) >= rank
+        z = z + jnp.where(later, split_dot_right(g0, both[tok:]), 0.0)
+        gsrc[...] = (z / (1.0 + jnp.exp(-z))).astype(BF16)
         for shift in (1, 2):
             for dc, e in slots:
                 g_copies.append(
                     send(gsrc, gbuf.at[shift - 1, dc * 2 + e], sec(shift), rep(dc, e))
                 )
 
-    def work4():
-        held["w3p"] = gather_pass(2, held["w3"])
-
     def work5():
         across["u", 0, 0].wait_recv()
         across["u", 1, 0].wait_recv()
-        held["own2"] = keep(upbuf.at[1, span1, :, inner], wfull.at[1, :, piece(r)])
+        held["own2"] = keep(upbuf.at[1, span1, :, inner], bleft.at[pl.ds(rank, rank), piece(r)])
         held["w2"] = gather_start(1, upbuf.at[1, span1, :, inner])
         late2, late1 = backward_span(after, 2, n), backward_span(after, 1, n)
         first = keep(upbuf.at[1, late2, :, inner], msrc.at[0])
@@ -257,16 +260,18 @@
 
     def work6():
         held["w2p"] = gather_pass(1, held["w2"])
+
+    def work7():
         gather_end(held["w3"], held["w3p"])
+        gather_end(held["w2"], held["w2p"])
         held["own3"].wait()
-        n2 = long_dot(wfull.at[2], down_v.at[1], tile)
-        held["a2"] = long_dot(wfull.at[2], ret_v, tile) + split_dot_left(n2, held["dz0"])
-
-    def work7():
-        gather_end(held["w2"], held["w2p"])
         held["own2"].wait()
-        n1 = long_dot(wfull.at[1], down_v.at[1], tile)
-        a1 = long_dot(wfull.at[1], ret_v, tile) + split_dot_left(n1, held["dz0"])
+        both = long_dot(bleft, bright, tile)
+        a0, a1, a2 = [both[i * rank : (i + 1) * rank, 0:tok] for i in range(3)]
+        _, n1, n2 = [both[i * rank : (i + 1) * rank, tok : tok + rank] for i in range(3)]
+        dz0 = (a0 * gate(stash_v[0])).astype(BF16)
+        csrc[0] = dot_nt(dz0, dz0)
+        a1 = a1 + split_dot_left(n1, dz0)
         st1.wait_recv()
         dz1 = (a1 * gate(stash_v[1])).astype(BF16)
         csrc[1] = dot_nt(dz1, dz1)
@@ -275,7 +280,7 @@
         n3 = mbuf[0]
         for d in range(1, reps):
             n3 = n3 + mbuf[d]
-        a2 = held["a2"] + split_dot_left(n3, dz1)
+        a2 = a2 + split_dot_left(n2, dz0) + split_dot_left(n3, dz1)
         st2.wait_recv()
         dz2 = (a2 * gate(stash_v[2])).astype(BF16)
         csrc[2] = dot_nt(dz2, dz2)
@@ -291,8 +296,8 @@
     works = [work0, work1, work2, work3, work4, work5, work6, work7]
     for at in range(len(pieces)):
         ahead[at].wait_recv()
-        if at + 2 < len(pieces):
-            send_ahead(at + 2)
+        if at + window < len(pieces):
+            send_ahead(at + window)
         if at == 0:
             works[0]()
             send_across(at)
@@ -330,12 +335,11 @@
         in_specs=[anywhere] * 6,
         out_specs=(anywhere,) * 5,
         scratch_shapes=[
-            pltpu.VMEM((tok, width), BF16),
-            pltpu.VMEM((tok, width), BF16),
-            pltpu.VMEM((2, rank, width), BF16),
-            pltpu.VMEM((2, rank, width), BF16),
+            pltpu.VMEM((tok + rank, width), BF16),
+            pltpu.VMEM((2 * rank, width), BF16),
+            pltpu.VMEM((3 * rank, width), BF16),
+            pltpu.VMEM((tok + rank, width), BF16),
             pltpu.VMEM((3, rank, tok), F32),
-            pltpu.VMEM((3, rank, width), BF16),
             pltpu.VMEM((tok, 2 * rank), BF16),
             pltpu.VMEM((2, rank, width // reps), BF16),
             pltpu.VMEM((reps + 1, rank, rank), F32),

time: 128 us -> 128 us (level)
  no operation moved by 1% of the time
where the time goes in v3:
time: 128 us; the launch traced here: 127 us
  Pallas kernels  122 us (95%)
  local copies, waits for them, and re-layouts  2.55 us (2%)
  other arithmetic  2.23 us (2%)
    pallas_call x1, Pallas kernels, exchange(): pl.pallas_call(functools.partial(exchange_kernel, n, reps, parts), out_sh...  104 us
    pallas_call x1, Pallas kernels, update_factor(): pl.pallas_call(functools.partial(factor_kernel, n, reps, 0.25 / (3 * toke...  17.7 us

profile of v3, /device:TPU:0, one launch (start us, length us, event | category | flops | bytes accessed | tf_op | source)
XLA Modules:
  0.0 127.4 jit_solution(9009299475952503619)
XLA Ops:
  0.7 0.1 fusion.10
  0.8 0.0 copy-start
  0.9 104.2 %exchange.1 = (bf16[3,4,128,2048]{3,2,1,0:T(8,128)(2,1)}, bf16[3,2,64,2048]{3,2,1,0:T(8,128)(2,1)}, bf16[2,4,128,128]{3,2,1,0:T(8,128)(2,1)}, s32[4,8,128]{2,1,0:T(8,128)}, f32[3,4,64,64]{3,2,1,0:T(8,128)}) custom-call(bf16[128,8192]{1,0:T(8,128)(2,1)} %bitcast.36, bf16[128,8192]{1,0:T(8,128)(2,1)} %bitcast.37, bf16[2,64,8192]{2,1,0:T(8,128)(2,1)} %bitcast.38, ...), custom_call_target="tpu_custom_call" | custom-call | tf_op jit(solution)/shard_map/exchange/pallas_call | solution.py:326
  105.1 0.7 copy.12
  105.8 0.6 gather_fusion
  106.4 0.1 select_bitcast_fusion
  106.5 0.1 fusion.11
  106.6 1.0 reduce_sum.48
  107.7 0.1 multiply_reduce_fusion
  107.8 0.0 copy-done
  107.8 0.7 fusion.5
  108.5 1.2 copy.13.weight
  109.7 17.7 %factor.1 = f32[2048,1024]{1,0:T(8,128)} custom-call(bf16[3,512,2048]{2,1,0:T(8,128)(2,1)} %bitcast.35, bf16[3,2,64,2048]{3,2,1,0:T(8,128)(2,1)} %get-tuple-element.8.upbuf, bf16[2,512,128]{2,1,0:T(8,128)(2,1)} %bitcast.40, f32[3,512,1]{2,1,0:T(8,128)} %copy.13.weight, f32[2048,1024]{1,0:T(8,128)} %bitcast.33), custom_call_target="tpu_custom_call" | custom-call | tf_op jit(solution)/shard_map/factor/pallas_call | solution.py:411
  (9 shorter events, 0.1 us)
Async XLA Ops:
  0.8 106.9 %copy-start = (f32[2,1,64,64]{3,2,1,0:T(8,128)S(1)}, f32[2,1,64,64]{3,2,1,0:T(8,128)}, u32[]{:S(2)}) copy-start(f32[2,1,64,64]{3,2,1,0:T(8,128)} %param.15) | copy-start | bytes 98308

commit v4 on v3

--- a/solution.py
+++ b/solution.py
@@ -53,8 +53,9 @@
 
 def exchange_kernel(
     n, reps, parts,
-    ent, ret, down, up, stash, docs,
-    buf, upbuf, gbuf, docbuf, cbuf,
+    ent, ret, down, up, stash, docs, old,
+    base, tail, cbuf,
+    buf, upbuf, gbuf, docbuf, weight, rows, total,
     fleft, fright, bleft, bright, stash_v, gsrc, msrc, mbuf, csrc,
     local_sem, send_sem, recv_sem,
 ):
@@ -119,6 +120,7 @@
     own_chunk = keep(ent.at[:, cols(r)], buf.at[0, 0])
     own_up = keep(up.at[:, :, cols(r)], upbuf.at[0])
     own_docs = keep(docs, docbuf.at[0])
+    load_old = keep(old, total)
 
     barrier = pltpu.get_barrier_semaphore()
     peers = 0
@@ -142,7 +144,6 @@
     ]
     inside, ahead, across = {}, {}, {}
     arrived = set()
-    window = 3
     odd = s % 2
     partner = s + 1 - 2 * odd
 
@@ -169,7 +170,7 @@
             src, dst = buf.at[2 * odd, d, bands[b]], buf.at[1, d, bands[b]]
         across[kind, d, b] = send(src, dst, partner, r)
 
-    for at in range(window):
+    for at in range(2 * parts):
         send_ahead(at)
     prev = sec(-1)
     w1_piece = send(
@@ -207,6 +208,71 @@
     def gate(q):
         sigma = 1.0 / (1.0 + jnp.exp(-q))
         return sigma * (1.0 + q * (1.0 - sigma))
+
+    block = total.shape[1]
+    height = min(256, share)
+    scale = 0.25 / (3 * tok * reps)
+
+    def weigh():
+        own_docs.wait()
+        for copy in doc_copies:
+            copy.wait_recv()
+        ids = docbuf[...]
+        length = jnp.zeros(ids.shape, F32)
+        for doc in range(2 * reps):
+            same = jnp.where(ids == doc, 1.0, 0.0)
+            count = jnp.sum(jnp.sum(same, axis=0), axis=1, keepdims=True)
+            length = length + same * count[None]
+        weight[...] = jnp.sqrt(jnp.sqrt(tok / length))
+
+    def column(slot, d):
+        own = weight[d]
+        mine = lax.broadcasted_iota(jnp.int32, own.shape, 0) == sec(-slot)
+        line = jnp.sum(jnp.where(mine, own, 0.0), axis=0, keepdims=True)
+        square = jnp.broadcast_to(line, (tok, tok))
+        across_, along = [lax.broadcasted_iota(jnp.int32, (tok, tok), i) for i in (0, 1)]
+        return jnp.sum(jnp.where(across_ == along, square, 0.0), axis=1, keepdims=True)
+
+    back1, back2 = sec(-1), sec(-2)
+    first1, _ = forward_spans(back1, n)
+    first2, second2 = forward_spans(back2, n)
+    strip = min(512, wide)
+
+    def form(slot, d, place):
+        scaled = column(slot, d)
+        here = pl.ds(place * tok, tok)
+
+        def fill(at, carry):
+            on = pl.ds(pl.multiple_of(at * strip, strip), strip)
+            act = buf[slot, d, :, on].astype(F32)
+            if slot == 1:
+                act = act + dot_nn(gbuf[0, d, :, 0:rank], upbuf[1, first1, :, on])
+                act = act.astype(BF16).astype(F32)
+            if slot == 2:
+                act = act + dot_nn(gbuf[1, d, :, 0:rank], upbuf[2, first2, :, on])
+                act = act.astype(BF16).astype(F32)
+                act = act + dot_nn(gbuf[1, d, :, rank : 2 * rank], upbuf[1, second2, :, on])
+                act = act.astype(BF16).astype(F32)
+            rows[here, on] = (scaled * act).astype(BF16)
+            return carry
+
+        lax.fori_loop(0, wide // strip, fill, 0)
+
+    def products(decay):
+        offset = r * share % wide
+
+        def one(at, carry):
+            left = pl.multiple_of(offset + at * height, 128)
+            right = pl.multiple_of(left // block * block, block)
+            here = pl.ds(pl.multiple_of(at * height, height), height)
+            gram = lax.dot_general(
+                rows[:, pl.ds(left, height)], rows[:, pl.ds(right, block)], DOWNWARD,
+                preferred_element_type=F32,
+            )
+            total[here] = decay * total[here] + gram * scale
+            return carry
+
+        lax.fori_loop(0, share // height, one, 0)
 
     held = {}
     g_copies, m_copies, c_copies = [], [], []
@@ -294,31 +360,70 @@
                 )
 
     works = [work0, work1, work2, work3, work4, work5, work6, work7]
+    started = set(range(2 * parts))
+
+    def arrive(d):
+        for at, (kind, of, _) in enumerate(pieces):
+            if kind == "e" and of == d and at not in started:
+                started.add(at)
+                send_ahead(at)
+
+    def own_products(start):
+        for d in range(start, start + 4):
+            form(0, d, d - start)
+        products(0.75 if start == 0 else 1.0)
+
+    def relayed(start):
+        for place, (slot, d) in enumerate([(1, start), (2, start), (1, start + 1), (2, start + 1)]):
+            form(slot, d, place)
+
+    waited = set()
+
+    def wait_across(d):
+        for b in range(parts):
+            if (d, b) not in waited:
+                waited.add((d, b))
+                across["e", d, b].wait_recv()
+
     for at in range(len(pieces)):
+        if at == 1:
+            arrive(1)
+        if at == 3:
+            for d in range(2, reps):
+                arrive(d)
         ahead[at].wait_recv()
-        if at + window < len(pieces):
-            send_ahead(at + window)
         if at == 0:
             works[0]()
-            send_across(at)
-            continue
         send_across(at)
-        if at < len(works):
+        if 0 < at < len(works):
             works[at]()
-
-    own_docs.wait()
+        if at == 4:
+            weigh()
+            load_old.wait()
+            own_products(0)
+    for start in range(4, reps, 4):
+        own_products(start)
+    for copy in g_copies:
+        copy.wait_recv()
+    for start in range(0, reps, 2):
+        wait_across(start)
+        wait_across(start + 1)
+        relayed(start)
+        if start + 2 < reps:
+            products(1.0)
+    write_base = keep(total, base)
+    write_tail = keep(rows, tail)
     held["own_c"].wait()
-    for copy in doc_copies + g_copies + c_copies:
+    for copy in c_copies:
         copy.wait_recv()
-    for (kind, _, _), copy in across.items():
-        if kind == "e":
-            copy.wait_recv()
+    write_base.wait()
+    write_tail.wait()
     for copy in copies:
         copy.wait_send()
     assert counts["copy"] <= send_sem.shape[0] and counts["local"] <= local_sem.shape[0]
 
 
-def exchange(ent, ret, down, up, stash, docs, n, reps, wide, parts):
+def exchange(ent, ret, down, up, stash, docs, old, n, reps, wide, parts):
     tok, width = ent.shape
     rank = up.shape[1]
     slots = 140 if reps <= 4 else 60 * reps
@@ -326,15 +431,20 @@
     return pl.pallas_call(
         functools.partial(exchange_kernel, n, reps, parts),
         out_shape=(
-            jax.ShapeDtypeStruct((3, reps, tok, wide), BF16),
-            jax.ShapeDtypeStruct((3, 2, rank, wide), BF16),
-            jax.ShapeDtypeStruct((2, reps, tok, 2 * rank), BF16),
-            jax.ShapeDtypeStruct((reps,) + docs.shape, jnp.int32),
+            jax.ShapeDtypeStruct(old.shape, F32),
+            jax.ShapeDtypeStruct((4 * tok, wide), BF16),
             jax.ShapeDtypeStruct((3, reps, rank, rank), F32),
         ),
-        in_specs=[anywhere] * 6,
-        out_specs=(anywhere,) * 5,
+        in_specs=[anywhere] * 7,
+        out_specs=(anywhere,) * 3,
         scratch_shapes=[
+            pltpu.VMEM((3, reps, tok, wide), BF16),
+            pltpu.VMEM((3, 2, rank, wide), BF16),
+            pltpu.VMEM((2, reps, tok, 2 * rank), BF16),
+            pltpu.VMEM((reps,) + docs.shape, jnp.int32),
+            pltpu.VMEM((reps,) + docs.shape, F32),
+            pltpu.VMEM((4 * tok, wide), BF16),
+            pltpu.VMEM(old.shape, F32),
             pltpu.VMEM((tok + rank, width), BF16),
             pltpu.VMEM((2 * rank, width), BF16),
             pltpu.VMEM((3 * rank, width), BF16),
@@ -344,7 +454,7 @@
             pltpu.VMEM((2, rank, width // reps), BF16),
             pltpu.VMEM((reps + 1, rank, rank), F32),
             pltpu.VMEM((3, rank, rank), F32),
-            pltpu.SemaphoreType.DMA((16,)),
+            pltpu.SemaphoreType.DMA((24,)),
             pltpu.SemaphoreType.DMA((slots,)),
             pltpu.SemaphoreType.DMA((slots,)),
         ],
@@ -352,108 +462,74 @@
             collective_id=0, has_side_effects=True, vmem_limit_bytes=63 * 1024 * 1024
         ),
         name="exchange",
-    )(ent, ret, down, up, stash, docs)
-
-
-def factor_kernel(n, reps, scale, buf, upbuf, gbuf, weight, old, new, rows):
+    )(ent, ret, down, up, stash, docs, old)
+
+
+def factor_kernel(n, reps, base_rows, scale, tokens, rows, cbuf, outer, base, new, outer_new):
     s = lax.axis_index("section")
     r = lax.axis_index("dp")
     step = pl.program_id(0)
-    _, tokens, wide = buf.shape
-    rank = upbuf.shape[2]
-    height, block = old.shape
-    share = height * pl.num_programs(0)
-
-    @pl.when(step == 0)
-    def _():
-        piece = min(512, wide)
-        back1, back2 = (s - 1 + n) % n, (s - 2 + n) % n
-        first1, _ = forward_spans(back1, n)
-        first2, second2 = forward_spans(back2, n)
-
-        def fill(at, carry):
-            here = pl.ds(pl.multiple_of(at * piece, piece), piece)
-            rows[0:tokens, here] = (weight[0] * buf[0, :, here].astype(F32)).astype(BF16)
-            act = buf[1, :, here].astype(F32) + dot_nn(
-                gbuf[0, :, 0:rank], upbuf[1, first1, :, here]
-            )
-            act = act.astype(BF16).astype(F32)
-            rows[tokens : 2 * tokens, here] = (weight[1] * act).astype(BF16)
-            act = buf[2, :, here].astype(F32) + dot_nn(
-                gbuf[1, :, 0:rank], upbuf[2, first2, :, here]
-            )
-            act = act.astype(BF16).astype(F32) + dot_nn(
-                gbuf[1, :, rank : 2 * rank], upbuf[1, second2, :, here]
-            )
-            act = act.astype(BF16).astype(F32)
-            rows[2 * tokens : 3 * tokens, here] = (weight[2] * act).astype(BF16)
-            return carry
-
-        lax.fori_loop(0, wide // piece, fill, 0)
-
-    width = share * reps
-    inside = (r * (width // reps)) % wide if width // reps < wide else 0
+    wide = rows.shape[1]
+    height, block = base.shape
+    share = base_rows
+    inside = (r * share) % wide if share < wide else 0
     left = pl.multiple_of(inside + step * height, 128)
     right = pl.multiple_of(left // block * block, block)
     total = lax.dot_general(
         rows[:, pl.ds(left, height)], rows[:, pl.ds(right, block)], DOWNWARD,
         preferred_element_type=F32,
     )
-    new[...] = 0.75 * old[...] + total * scale
-
-
-def update_factor(buf, upbuf, gbuf, weight, old, n, reps):
-    share, block = old.shape
-    _, tokens, wide = buf.shape
+    new[...] = base[...] + total * scale
+
+    @pl.when(step == 0)
+    def _():
+        for span in range(2):
+            sums = jnp.zeros(outer.shape[1:], F32)
+            held = jnp.int32(0)
+            for at in range(3):
+                second = 1 - (s + at) // n
+                member = second if span == 1 else 1 - second
+                curv = cbuf[at, 0]
+                for d in range(1, reps):
+                    curv = curv + cbuf[at, d]
+                sums = sums + jnp.where(member == 1, curv, 0.0)
+                held = held + member
+            divisor = jnp.maximum(held, 1).astype(F32) * tokens
+            updated = 0.75 * outer[span] + 0.25 * sums / divisor
+            outer_new[span] = jnp.where(held > 0, updated, outer[span])
+
+
+def update_factor(rows, cbuf, outer, base, n, reps, tokens):
+    share, block = base.shape
     height = min(256, share)
     whole = pl.BlockSpec(memory_space=pltpu.VMEM)
     tile = pl.BlockSpec((height, block), lambda i: (i, 0))
     return pl.pallas_call(
-        functools.partial(factor_kernel, n, reps, 0.25 / (3 * tokens)),
-        out_shape=jax.ShapeDtypeStruct(old.shape, F32),
+        functools.partial(factor_kernel, n, reps, share, 0.25 / (3 * tokens), tokens),
+        out_shape=(
+            jax.ShapeDtypeStruct(base.shape, F32), jax.ShapeDtypeStruct(outer.shape, F32)
+        ),
         grid=(share // height,),
-        in_specs=[whole, whole, whole, whole, tile],
-        out_specs=tile,
-        scratch_shapes=[pltpu.VMEM((3 * tokens, wide), BF16)],
+        in_specs=[whole, whole, whole, tile],
+        out_specs=(tile, pl.BlockSpec(outer.shape, lambda i: (0, 0, 0))),
         compiler_params=pltpu.CompilerParams(vmem_limit_bytes=63 * 1024 * 1024),
         name="factor",
-    )(buf, upbuf, gbuf, weight, old)
+    )(rows, cbuf, outer, base)
 
 
 def shards(
     entering, returning, adapter_down, adapter_up, stashed, doc_ids, input_factor, output_factor
 ):
-    s = lax.axis_index("section")
     n = lax.axis_size("section")
     reps = lax.axis_size("dp")
     tok, width = entering.shape[1:]
     block = input_factor.shape[2]
-    steps = stashed.shape[1]
-    rank = stashed.shape[2]
-    tokens = tok * reps
     wide = max(block, width // reps)
-    buf, upbuf, gbuf, docbuf, cbuf = exchange(
+    base, tail, cbuf = exchange(
         entering[0], returning[0], adapter_down[:, 0], adapter_up[:, 0], stashed[0], doc_ids,
-        n, reps, wide, 2,
+        input_factor[0], n, reps, wide, 2,
     )
-    anchors = (s - jnp.arange(steps, dtype=jnp.int32)) % n
-    mine = jnp.take(docbuf, anchors, axis=1).transpose(1, 0, 2).reshape(steps, tokens)
-    same = mine[:, :, None] == jnp.arange(2 * reps, dtype=jnp.int32)
-    counts = jnp.sum(same.astype(F32), axis=1)
-    length = jnp.sum(jnp.where(same, counts[:, None, :], 0.0), axis=2)
-    weight = jnp.sqrt(jnp.sqrt(tok / length))[:, :, None]
-    factor = update_factor(
-        buf.reshape(steps, tokens, wide), upbuf, gbuf.reshape(2, tokens, 2 * rank), weight,
-        input_factor[0], n, reps,
-    )
-    curv = jnp.sum(cbuf, axis=1)
-    second = (s + jnp.arange(steps) < n).astype(F32)
-    member = jnp.stack([1.0 - second, second])
-    held = jnp.sum(member, axis=1)
-    total = jnp.sum(member[:, :, None, None] * curv[None], axis=1)
-    divisor = (jnp.maximum(held, 1.0) * tokens)[:, None, None]
-    updated = 0.75 * output_factor[:, 0] + 0.25 * total / divisor
-    outer = jnp.where((held > 0.0)[:, None, None], updated, output_factor[:, 0])
+    factor, outer = update_factor(tail, cbuf, output_factor[:, 0], base, n, reps, tok * reps)
     return factor[None], outer[:, None]
 
 

time: 128 us -> 124 us (0.969)
  local copies, waits for them, and re-layouts: 2.55 us -> 0 us
  other arithmetic: 2.23 us -> 0 us
    pallas_call x1, Pallas kernels: 104 us -> 112 us  [exchange(): pl.pallas_call(functools.partial(exchange_kernel, n, reps, parts), out_sh...]
    pallas_call x1, Pallas kernels: 17.7 us -> 11.5 us  [update_factor(): pl.pallas_call(functools.partial(factor_kernel, n, reps, share, 0.25 / (3...]
where the time goes in v4:
time: 124 us
  Pallas kernels  123 us (99%)
    pallas_call x1, Pallas kernels, exchange(): pl.pallas_call(functools.partial(exchange_kernel, n, reps, parts), out_sh...  112 us
    pallas_call x1, Pallas kernels, update_factor(): pl.pallas_call(functools.partial(factor_kernel, n, reps, share, 0.25 / (3...  11.5 us

profile of v4, /device:TPU:0, one launch (start us, length us, event | category | flops | bytes accessed | tf_op | source)
XLA Modules:
  0.0 123.9 jit_solution(17706498057777879507)
XLA Ops:
  0.6 111.8 %exchange.1 = (f32[2048,1024]{1,0:T(8,128)}, bf16[512,2048]{1,0:T(8,128)(2,1)}, f32[3,4,64,64]{3,2,1,0:T(8,128)}) custom-call(bf16[128,8192]{1,0:T(8,128)(2,1)} %bitcast.12, bf16[128,8192]{1,0:T(8,128)(2,1)} %bitcast.13, bf16[2,64,8192]{2,1,0:T(8,128)(2,1)} %bitcast.14, bf16[2,64,8192]{2,1,0:T(8,128)(2,1)} %bitcast.15, f32[3,64,128]{2,1,0:T(8,128)} %bitcast.16, ...), custom_call_target="tpu_custom_call" | custom-call | tf_op jit(solution)/shard_map/exchange/pallas_call | solution.py:431
  112.4 11.5 %factor.1 = (f32[2048,1024]{1,0:T(8,128)}, f32[2,64,64]{2,1,0:T(8,128)}) custom-call(bf16[512,2048]{1,0:T(8,128)(2,1)} %get-tuple-element.7.rows, f32[3,4,64,64]{3,2,1,0:T(8,128)} %get-tuple-element.8.cbuf, f32[2,64,64]{2,1,0:T(8,128)} %bitcast.17, f32[2048,1024]{1,0:T(8,128)} %get-tuple-element.9.base), custom_call_target="tpu_custom_call" | custom-call | tf_op jit(solution)/shard_map/factor/pallas_call | solution.py:507

commit v5 on v4

--- a/solution.py
+++ b/solution.py
@@ -373,10 +373,6 @@
             form(0, d, d - start)
         products(0.75 if start == 0 else 1.0)
 
-    def relayed(start):
-        for place, (slot, d) in enumerate([(1, start), (2, start), (1, start + 1), (2, start + 1)]):
-            form(slot, d, place)
-
     waited = set()
 
     def wait_across(d):
@@ -384,6 +380,16 @@
             if (d, b) not in waited:
                 waited.add((d, b))
                 across["e", d, b].wait_recv()
+
+    def relay(start):
+        if start == 0:
+            for copy in g_copies:
+                copy.wait_recv()
+        wait_across(start)
+        wait_across(start + 1)
+        for place, (slot, d) in enumerate([(1, start), (2, start), (1, start + 1), (2, start + 1)]):
+            form(slot, d, place)
+        products(1.0)
 
     for at in range(len(pieces)):
         if at == 1:
@@ -401,23 +407,29 @@
             weigh()
             load_old.wait()
             own_products(0)
+        if at == 8:
+            relay(0)
     for start in range(4, reps, 4):
         own_products(start)
-    for copy in g_copies:
-        copy.wait_recv()
-    for start in range(0, reps, 2):
-        wait_across(start)
-        wait_across(start + 1)
-        relayed(start)
-        if start + 2 < reps:
-            products(1.0)
-    write_base = keep(total, base)
-    write_tail = keep(rows, tail)
+    for start in range(2, reps - 2, 2):
+        relay(start)
+    quarter = share // 4
+    writes = [
+        keep(total.at[pl.ds(i * quarter, quarter)], base.at[pl.ds(i * quarter, quarter)])
+        for i in range(4)
+    ]
+    for d in (reps - 2, reps - 1):
+        place = 2 * (d - reps + 2)
+        wait_across(d)
+        form(1, d, place)
+        form(2, d, place + 1)
+        done = pl.ds(place * tok, 2 * tok)
+        writes.append(keep(rows.at[done], tail.at[done]))
     held["own_c"].wait()
     for copy in c_copies:
         copy.wait_recv()
-    write_base.wait()
-    write_tail.wait()
+    for write in writes:
+        write.wait()
     for copy in copies:
         copy.wait_send()
     assert counts["copy"] <= send_sem.shape[0] and counts["local"] <= local_sem.shape[0]
@@ -454,7 +466,7 @@
             pltpu.VMEM((2, rank, width // reps), BF16),
             pltpu.VMEM((reps + 1, rank, rank), F32),
             pltpu.VMEM((3, rank, rank), F32),
-            pltpu.SemaphoreType.DMA((24,)),
+            pltpu.SemaphoreType.DMA((32,)),
             pltpu.SemaphoreType.DMA((slots,)),
             pltpu.SemaphoreType.DMA((slots,)),
         ],
@@ -465,21 +477,28 @@
     )(ent, ret, down, up, stash, docs, old)
 
 
-def factor_kernel(n, reps, base_rows, scale, tokens, rows, cbuf, outer, base, new, outer_new):
+def factor_kernel(
+    n, reps, base_rows, scale, tokens, upper, lower, cbuf, outer, base, base2, new, outer_new
+):
     s = lax.axis_index("section")
     r = lax.axis_index("dp")
     step = pl.program_id(0)
-    wide = rows.shape[1]
-    height, block = base.shape
+    wide = upper.shape[1]
+    height, block = new.shape
     share = base_rows
     inside = (r * share) % wide if share < wide else 0
     left = pl.multiple_of(inside + step * height, 128)
     right = pl.multiple_of(left // block * block, block)
-    total = lax.dot_general(
-        rows[:, pl.ds(left, height)], rows[:, pl.ds(right, block)], DOWNWARD,
-        preferred_element_type=F32,
-    )
-    new[...] = base[...] + total * scale
+    half = block // 2
+    for at, old in enumerate((base, base2)):
+        here = pl.ds(pl.multiple_of(right + at * half, 128), half)
+        total = jnp.zeros((height, half), F32)
+        for rows in (upper, lower):
+            total = total + lax.dot_general(
+                rows[:, pl.ds(left, height)], rows[:, here], DOWNWARD,
+                preferred_element_type=F32,
+            )
+        new[:, at * half : (at + 1) * half] = old[...] + total * scale
 
     @pl.when(step == 0)
     def _():
@@ -510,11 +529,17 @@
             jax.ShapeDtypeStruct(base.shape, F32), jax.ShapeDtypeStruct(outer.shape, F32)
         ),
         grid=(share // height,),
-        in_specs=[whole, whole, whole, tile],
+        in_specs=[
+            pl.BlockSpec((rows.shape[0] // 2, rows.shape[1]), lambda i: (0, 0)),
+            pl.BlockSpec((rows.shape[0] // 2, rows.shape[1]), lambda i: (1, 0)),
+            whole, whole,
+            pl.BlockSpec((height, block // 2), lambda i: (i, 0)),
+            pl.BlockSpec((height, block // 2), lambda i: (i, 1)),
+        ],
         out_specs=(tile, pl.BlockSpec(outer.shape, lambda i: (0, 0, 0))),
         compiler_params=pltpu.CompilerParams(vmem_limit_bytes=63 * 1024 * 1024),
         name="factor",
-    )(rows, cbuf, outer, base)
+    )(rows, rows, cbuf, outer, base, base)
 
 
 def shards(

time: 124 us -> 120 us (0.968)
  Pallas kernels: 123 us -> 119 us
    pallas_call x1, Pallas kernels: 112 us -> 107 us  [exchange(): pl.pallas_call(functools.partial(exchange_kernel, n, reps, parts), out_sh...]
where the time goes in v5:
time: 120 us; the launch traced here: 119 us
  Pallas kernels  119 us (99%)
    pallas_call x1, Pallas kernels, exchange(): pl.pallas_call(functools.partial(exchange_kernel, n, reps, parts), out_sh...  107 us
    pallas_call x1, Pallas kernels, update_factor(): pl.pallas_call(functools.partial(factor_kernel, n, reps, share, 0.25 / (3...  11.3 us

profile of v5, /device:TPU:0, one launch (start us, length us, event | category | flops | bytes accessed | tf_op | source)
XLA Modules:
  0.0 119.2 jit_solution(6115000526386835838)
XLA Ops:
  0.6 107.2 %exchange.1 = (f32[2048,1024]{1,0:T(8,128)}, bf16[512,2048]{1,0:T(8,128)(2,1)}, f32[3,4,64,64]{3,2,1,0:T(8,128)}) custom-call(bf16[128,8192]{1,0:T(8,128)(2,1)} %bitcast.12, bf16[128,8192]{1,0:T(8,128)(2,1)} %bitcast.13, bf16[2,64,8192]{2,1,0:T(8,128)(2,1)} %bitcast.14, bf16[2,64,8192]{2,1,0:T(8,128)(2,1)} %bitcast.15, f32[3,64,128]{2,1,0:T(8,128)} %bitcast.16, ...), custom_call_target="tpu_custom_call" | custom-call | tf_op jit(solution)/shard_map/exchange/pallas_call | solution.py:443
  107.9 11.3 %factor.1 = (f32[2048,1024]{1,0:T(8,128)}, f32[2,64,64]{2,1,0:T(8,128)}) custom-call(bf16[512,2048]{1,0:T(8,128)(2,1)} %get-tuple-element.7.upper.lower, bf16[512,2048]{1,0:T(8,128)(2,1)} %get-tuple-element.7.upper.lower, f32[3,4,64,64]{3,2,1,0:T(8,128)} %get-tuple-element.8.cbuf, f32[2,64,64]{2,1,0:T(8,128)} %bitcast.17, ...), custom_call_target="tpu_custom_call" | custom-call | tf_op jit(solution)/shard_map/factor/pallas_call | solution.py:526

commit v6 on v5

--- a/solution.py
+++ b/solution.py
@@ -150,11 +150,11 @@
     def send_ahead(at):
         kind, d, b = pieces[at]
         if kind == "u":
-            src, dst = up.at[d, :, cols(r)], upbuf.at[2, d]
+            src, dst = upbuf.at[0, d], upbuf.at[2, d]
         else:
             dst = buf.at[2, d, bands[b]]
             if d == 0:
-                src = ent.at[bands[b], cols(r)]
+                src = fleft.at[bands[b], cols(r)]
             else:
                 src = buf.at[0, d, bands[b]]
                 if d not in arrived:
@@ -170,6 +170,8 @@
             src, dst = buf.at[2 * odd, d, bands[b]], buf.at[1, d, bands[b]]
         across[kind, d, b] = send(src, dst, partner, r)
 
+    forward_loads[0].wait()
+    own_up.wait()
     for at in range(2 * parts):
         send_ahead(at)
     prev = sec(-1)
@@ -178,7 +180,9 @@
     )
     for dc, e in slots[1:]:
         target = rep(dc, e)
-        inside[dc, e] = send(ent.at[:, cols(target)], buf.at[0, dc * 2 + e], s, target)
+        inside[dc, e] = send(
+            fleft.at[pl.ds(0, tok), cols(target)], buf.at[0, dc * 2 + e], s, target
+        )
     doc_copies = [send(docs, docbuf.at[dc * 2 + e], s, rep(dc, e)) for dc, e in slots[1:]]
     st1 = send(stash.at[1], stash_v.at[1], sec(1), r)
     st2 = send(stash.at[2], stash_v.at[2], sec(2), r)
@@ -281,12 +285,11 @@
 
     def work0():
         own_chunk.wait()
-        own_up.wait()
         w1_piece.wait_recv()
         held["w1"] = gather_start(0, fright.at[pl.ds(rank, rank), piece(r)])
 
     def work1():
-        for load in forward_loads + backward_loads:
+        for load in forward_loads[1:] + backward_loads:
             load.wait()
 
     def work2():

time: 120 us -> 120 us (level)
  no operation moved by 1% of the time
where the time goes in v6:
time: 120 us
  Pallas kernels  119 us (99%)
    pallas_call x1, Pallas kernels, exchange(): pl.pallas_call(functools.partial(exchange_kernel, n, reps, parts), out_sh...  108 us
    pallas_call x1, Pallas kernels, update_factor(): pl.pallas_call(functools.partial(factor_kernel, n, reps, share, 0.25 / (3...  11.3 us

profile of v6, /device:TPU:0, one launch (start us, length us, event | category | flops | bytes accessed | tf_op | source)
XLA Modules:
  0.0 119.6 jit_solution(12244871538996015687)
XLA Ops:
  0.6 107.6 %exchange.1 = (f32[2048,1024]{1,0:T(8,128)}, bf16[512,2048]{1,0:T(8,128)(2,1)}, f32[3,4,64,64]{3,2,1,0:T(8,128)}) custom-call(bf16[128,8192]{1,0:T(8,128)(2,1)} %bitcast.12, bf16[128,8192]{1,0:T(8,128)(2,1)} %bitcast.13, bf16[2,64,8192]{2,1,0:T(8,128)(2,1)} %bitcast.14, bf16[2,64,8192]{2,1,0:T(8,128)(2,1)} %bitcast.15, f32[3,64,128]{2,1,0:T(8,128)} %bitcast.16, ...), custom_call_target="tpu_custom_call" | custom-call | tf_op jit(solution)/shard_map/exchange/pallas_call | solution.py:446
  108.2 11.3 %factor.1 = (f32[2048,1024]{1,0:T(8,128)}, f32[2,64,64]{2,1,0:T(8,128)}) custom-call(bf16[512,2048]{1,0:T(8,128)(2,1)} %get-tuple-element.7.upper.lower, bf16[512,2048]{1,0:T(8,128)(2,1)} %get-tuple-element.7.upper.lower, f32[3,4,64,64]{3,2,1,0:T(8,128)} %get-tuple-element.8.cbuf, f32[2,64,64]{2,1,0:T(8,128)} %bitcast.17, ...), custom_call_target="tpu_custom_call" | custom-call | tf_op jit(solution)/shard_map/factor/pallas_call | solution.py:529

commit v7 on v6

--- a/solution.py
+++ b/solution.py
@@ -523,7 +523,7 @@
 
 def update_factor(rows, cbuf, outer, base, n, reps, tokens):
     share, block = base.shape
-    height = min(256, share)
+    height = min(512, share)
     whole = pl.BlockSpec(memory_space=pltpu.VMEM)
     tile = pl.BlockSpec((height, block), lambda i: (i, 0))
     return pl.pallas_call(

time: 120 us -> 117 us (0.975)
  Pallas kernels: 119 us -> 117 us
    pallas_call x1, Pallas kernels: 11.3 us -> 9.03 us  [update_factor(): pl.pallas_call(functools.partial(factor_kernel, n, reps, share, 0.25 / (3...]
where the time goes in v7:
time: 117 us
  Pallas kernels  117 us (100%)
    pallas_call x1, Pallas kernels, exchange(): pl.pallas_call(functools.partial(exchange_kernel, n, reps, parts), out_sh...  108 us
    pallas_call x1, Pallas kernels, update_factor(): pl.pallas_call(functools.partial(factor_kernel, n, reps, share, 0.25 / (3...  9.03 us

profile of v7, /device:TPU:0, one launch (start us, length us, event | category | flops | bytes accessed | tf_op | source)
XLA Modules:
  0.0 117.3 jit_solution(10129541389174739460)
XLA Ops:
  0.6 107.6 %exchange.1 = (f32[2048,1024]{1,0:T(8,128)}, bf16[512,2048]{1,0:T(8,128)(2,1)}, f32[3,4,64,64]{3,2,1,0:T(8,128)}) custom-call(bf16[128,8192]{1,0:T(8,128)(2,1)} %bitcast.12, bf16[128,8192]{1,0:T(8,128)(2,1)} %bitcast.13, bf16[2,64,8192]{2,1,0:T(8,128)(2,1)} %bitcast.14, bf16[2,64,8192]{2,1,0:T(8,128)(2,1)} %bitcast.15, f32[3,64,128]{2,1,0:T(8,128)} %bitcast.16, ...), custom_call_target="tpu_custom_call" | custom-call | tf_op jit(solution)/shard_map/exchange/pallas_call | solution.py:446
  108.2 9.0 %factor.1 = (f32[2048,1024]{1,0:T(8,128)}, f32[2,64,64]{2,1,0:T(8,128)}) custom-call(bf16[512,2048]{1,0:T(8,128)(2,1)} %get-tuple-element.7.upper.lower, bf16[512,2048]{1,0:T(8,128)(2,1)} %get-tuple-element.7.upper.lower, f32[3,4,64,64]{3,2,1,0:T(8,128)} %get-tuple-element.8.cbuf, f32[2,64,64]{2,1,0:T(8,128)} %bitcast.17, ...), custom_call_target="tpu_custom_call" | custom-call | tf_op jit(solution)/shard_map/factor/pallas_call | solution.py:529
